TPU v7x, 32 devices: a whole 2x2x4 slice. The times are simulated.
32 devices in a mesh: section: 4 (over y, x), dp: 8 (over z, core).
Axes of the slice: x: 2, y: 2, z: 4, core: 2. Of those that a mesh axis runs over, the one named last changes fastest.
Arguments:
- inputs: bfloat16 [32, 32, 960], P('dp', None, 'section'), may hold values from -6 to 6
- cotangent: bfloat16 [32, 32, 960], P('dp', None, 'section'), may hold values from -6 to 6
- first_gain: float32 [4, 960], P('section'), may hold values from 0.5 to 1.5
- w_query: bfloat16 [4, 960, 960], P('section'), may hold values from -0.1875 to 0.1875
- w_key: bfloat16 [4, 960, 320], P('section'), may hold values from -0.1875 to 0.1875
- w_value: bfloat16 [4, 960, 320], P('section'), may hold values from -0.1875 to 0.1875
- w_output: bfloat16 [4, 960, 960], P('section'), may hold values from -0.5 to 0.5
- second_gain: float32 [4, 960], P('section'), may hold values from 0.5 to 1.5
- w_gate: bfloat16 [4, 960, 2560], P('section'), may hold values from -0.1875 to 0.1875
- w_up: bfloat16 [4, 960, 2560], P('section'), may hold values from -0.1875 to 0.1875
- w_down: bfloat16 [4, 2560, 960], P('section'), may hold values from -0.125 to 0.125
Outputs:
- section_outputs: float32 [32, 32, 960], P('dp', None, 'section')
- delta_inputs: float32 [32, 32, 960], P('dp', None, 'section')
- delta_first: float32 [4, 960], P('section', 'dp')
- delta_query: float32 [4, 960, 960], P('section', 'dp')
- delta_key: float32 [4, 960, 320], P('section', 'dp')
- delta_value: float32 [4, 960, 320], P('section', 'dp')
- delta_output: float32 [4, 960, 960], P('section', 'dp')
- delta_second: float32 [4, 960], P('section', 'dp')
- delta_gate: float32 [4, 960, 2560], P('section', 'dp')
- delta_up: float32 [4, 960, 2560], P('section', 'dp')
- delta_down: float32 [4, 2560, 960], P('section', None, 'dp')
- global_norm: float32 [], replicated
All inputs are finite; a program needn't handle non-finite values.
Results may differ from a plain program's by a relative error of at most 0.025.
Values may be sent and summed in bfloat16 or wider, within the bound.
No kernel may reach another device: no remote copies, remote signals or barrier semaphores. Data moves between devices by JAX's collectives and lax.ppermute only.
A program may use at most 256 MiB of HBM per device.

v0:
```python
import jax
import jax.numpy as jnp
from jax import lax
from jax.sharding import PartitionSpec as P

HEADS = 15
KV_HEADS = 5
HEAD = 64
FF = 2560


EPSILON = 1e-05
THETA = 10000.0


def from_behind(block, axis, distance):
    devices = range(lax.axis_size(axis))
    route = [(i - distance, i) for i in devices if i - distance in devices]
    return lax.ppermute(block, axis, route)


def rotate_half(tensor):
    half = tensor.shape[-1] // 2
    return jnp.concatenate([-tensor[..., half:], tensor[..., :half]], axis=-1)


def rotary_tables(length):
    half = HEAD // 2
    frequency = THETA ** (-(jnp.arange(half, dtype=jnp.float32) * 2.0 / HEAD))
    angles = jnp.arange(length, dtype=jnp.float32)[:, None] * frequency[None, :]
    angles = jnp.concatenate([angles, angles], axis=-1)
    return (jnp.cos(angles)[:, None, :], jnp.sin(angles)[:, None, :])


def matmul(left, right):
    return jnp.dot(left, right, preferred_element_type=jnp.float32)


def transposed(left, right):
    return lax.dot_general(
        left, right, (((1,), (1,)), ((), ())), preferred_element_type=jnp.float32
    )


def outer_sum(left, right):
    return lax.dot_general(
        left, right, (((0,), (0,)), ((), ())), preferred_element_type=jnp.float32
    )


def mean_scale(residual):
    return lax.rsqrt(jnp.mean(residual * residual, axis=-1, keepdims=True) + EPSILON)


def norm_back(slope, residual, scale, gain):
    shaped = slope * gain
    inner = jnp.mean(shaped * residual, axis=-1, keepdims=True)
    gain_term = jnp.sum(slope * residual * scale, axis=0)
    return (scale * shaped - residual * scale * scale * scale * inner, gain_term)


def block_forward(residual, weights, tables):
    first_gain, w_query, w_key, w_value, w_output, second_gain, w_gate, w_up, w_down = weights
    cosine, sine, causal = tables
    length, width = residual.shape
    group = HEADS // KV_HEADS
    first_scale = mean_scale(residual)
    normed = (residual * first_scale * first_gain).astype(jnp.bfloat16)
    query = matmul(normed, w_query).reshape(length, HEADS, HEAD)
    keys = matmul(normed, w_key).reshape(length, KV_HEADS, HEAD)
    values = matmul(normed, w_value).astype(jnp.bfloat16).reshape(length, KV_HEADS, HEAD)
    query_turned = (
        (query * cosine + rotate_half(query) * sine)
        .astype(jnp.bfloat16)
        .reshape(length, KV_HEADS, group, HEAD)
    )
    keys_turned = (keys * cosine + rotate_half(keys) * sine).astype(jnp.bfloat16)
    scores = jnp.einsum(
        "qgrd,kgd->grqk", query_turned, keys_turned, preferred_element_type=jnp.float32
    ) * HEAD ** (-0.5)
    scores = jnp.where(causal, scores, -1e30)
    highest = jnp.max(scores, axis=-1, keepdims=True)
    log_total = highest + jnp.log(jnp.sum(jnp.exp(scores - highest), axis=-1, keepdims=True))
    chances = jnp.exp(scores - log_total).astype(jnp.bfloat16)
    context = jnp.einsum("grqk,kgd->qgrd", chances, values, preferred_element_type=jnp.float32)
    context = context.reshape(length, width).astype(jnp.bfloat16)
    middle = residual + matmul(context, w_output)
    second_scale = mean_scale(middle)
    second_normed = (middle * second_scale * second_gain).astype(jnp.bfloat16)
    gate = matmul(second_normed, w_gate)
    up = matmul(second_normed, w_up)
    activation = (gate * jax.nn.sigmoid(gate) * up).astype(jnp.bfloat16)
    result = middle + matmul(activation, w_down)
    kept = (
        residual,
        first_scale,
        normed,
        query_turned,
        keys_turned,
        values,
        log_total,
        context,
        middle,
        second_scale,
        second_normed,
        gate,
        up,
        activation,
    )
    return (result, kept)


def empty_kept(micro, length, width):
    group = HEADS // KV_HEADS
    shapes = (
        ((length, width), jnp.float32),
        ((length, 1), jnp.float32),
        ((length, width), jnp.bfloat16),
        ((length, KV_HEADS, group, HEAD), jnp.bfloat16),
        ((length, KV_HEADS, HEAD), jnp.bfloat16),
        ((length, KV_HEADS, HEAD), jnp.bfloat16),
        ((KV_HEADS, group, length, 1), jnp.float32),
        ((length, width), jnp.bfloat16),
        ((length, width), jnp.float32),
        ((length, 1), jnp.float32),
        ((length, width), jnp.bfloat16),
        ((length, FF), jnp.float32),
        ((length, FF), jnp.float32),
        ((length, FF), jnp.bfloat16),
    )
    return tuple((jnp.zeros((micro, 2) + shape, kind) for shape, kind in shapes))


def block_backward(slope, kept, weights, tables):
    first_gain, w_query, w_key, w_value, w_output, second_gain, w_gate, w_up, w_down = weights
    cosine, sine, causal = tables
    (
        residual,
        first_scale,
        normed,
        query_turned,
        keys_turned,
        values,
        log_total,
        context,
        middle,
        second_scale,
        second_normed,
        gate,
        up,
        activation,
    ) = kept
    length, width = residual.shape
    group = HEADS // KV_HEADS
    mixer_slope = slope.astype(jnp.bfloat16)
    active_slope = transposed(mixer_slope, w_down)
    sigma = jax.nn.sigmoid(gate)
    gate_slope = (active_slope * up * sigma * (1.0 + gate * (1.0 - sigma))).astype(jnp.bfloat16)
    up_slope = (active_slope * gate * sigma).astype(jnp.bfloat16)
    normed_slope = transposed(gate_slope, w_gate) + transposed(up_slope, w_up)
    middle_part, second_term = norm_back(normed_slope, middle, second_scale, second_gain)
    middle_slope = slope + middle_part
    branch_slope = middle_slope.astype(jnp.bfloat16)
    context_slope = transposed(branch_slope, w_output).astype(jnp.bfloat16)
    scores = jnp.einsum(
        "qgrd,kgd->grqk", query_turned, keys_turned, preferred_element_type=jnp.float32
    ) * HEAD ** (-0.5)
    scores = jnp.where(causal, scores, -1e30)
    chances = jnp.exp(scores - log_total)
    split_slope = context_slope.reshape(length, KV_HEADS, group, HEAD)
    chance_slope = jnp.einsum(
        "qgrd,kgd->grqk", split_slope, values, preferred_element_type=jnp.float32
    )
    inner = jnp.sum(chances * chance_slope, axis=-1, keepdims=True)
    score_slope = (chances * (chance_slope - inner)).astype(jnp.bfloat16)
    value_back = jnp.einsum(
        "grqk,qgrd->kgd",
        chances.astype(jnp.bfloat16),
        split_slope,
        preferred_element_type=jnp.float32,
    )
    query_back = jnp.einsum(
        "grqk,kgd->qgrd", score_slope, keys_turned, preferred_element_type=jnp.float32
    )
    query_back = query_back.reshape(length, HEADS, HEAD) * HEAD ** (-0.5)
    keys_back = jnp.einsum(
        "grqk,qgrd->kgd", score_slope, query_turned, preferred_element_type=jnp.float32
    ) * HEAD ** (-0.5)
    query_slope = (
        (query_back * cosine - rotate_half(query_back) * sine)
        .astype(jnp.bfloat16)
        .reshape(length, width)
    )
    keys_slope = (
        (keys_back * cosine - rotate_half(keys_back) * sine)
        .astype(jnp.bfloat16)
        .reshape(length, -1)
    )
    value_slope = value_back.astype(jnp.bfloat16).reshape(length, -1)
    first_slope = (
        transposed(query_slope, w_query)
        + transposed(keys_slope, w_key)
        + transposed(value_slope, w_value)
    )
    residual_part, first_term = norm_back(first_slope, residual, first_scale, first_gain)
    residual_slope = middle_slope + residual_part
    attend_slope = jnp.concatenate([query_slope, keys_slope, value_slope], axis=1)
    feed_slope = jnp.concatenate([gate_slope, up_slope], axis=1)
    pairs = (
        normed,
        attend_slope,
        context,
        branch_slope,
        second_normed,
        feed_slope,
        mixer_slope,
        activation,
    )
    return (residual_slope, (first_term, second_term), pairs)


def weight_parts(pairs):
    (
        normed,
        attend_slope,
        context,
        branch_slope,
        second_normed,
        feed_slope,
        mixer_slope,
        activation,
    ) = pairs
    return (
        outer_sum(normed, attend_slope),
        outer_sum(context, branch_slope),
        outer_sum(second_normed, feed_slope),
        outer_sum(mixer_slope, activation),
    )


def per_device(
    inputs,
    cotangent,
    first_gain,
    w_query,
    w_key,
    w_value,
    w_output,
    second_gain,
    w_gate,
    w_up,
    w_down,
):
    sections = lax.axis_size("section")
    section = lax.axis_index("section")
    weights = (
        first_gain[0],
        w_query[0],
        w_key[0],
        w_value[0],
        w_output[0],
        second_gain[0],
        w_gate[0],
        w_up[0],
        w_down[0],
    )
    whole_inputs, whole_cotangent = (
        lax.all_gather(inputs, "section", axis=2, tiled=True),
        lax.all_gather(cotangent, "section", axis=2, tiled=True),
    )
    micro, length, width = whole_inputs.shape
    pair_width = KV_HEADS * HEAD
    cosine, sine = rotary_tables(length)
    positions = jnp.arange(length)
    tables = (cosine, sine, positions[:, None] >= positions[None, :])
    ticks = micro + sections - 1

    def forward_tick(carry, tick):
        arriving, stash, final = carry
        micro_index = tick - section
        active = jnp.logical_and(micro_index >= 0, micro_index < micro)
        slot = jnp.clip(micro_index, 0, micro - 1)
        first = lax.dynamic_index_in_dim(whole_inputs, slot, 0, keepdims=False)
        entering = jnp.where(section == 0, first, arriving).astype(jnp.float32)

        def forward_run(state):
            stash, final = state
            between, kept_one = block_forward(entering, weights, tables)
            leaving, kept_two = block_forward(between, weights, tables)
            both = jax.tree.map(lambda one, two: jnp.stack([one, two]), kept_one, kept_two)
            stash = jax.tree.map(
                lambda store, item: lax.dynamic_update_index_in_dim(store, item, slot, 0),
                stash,
                both,
            )
            final = lax.dynamic_update_index_in_dim(
                final, jnp.where(section == sections - 1, leaving, 0.0), slot, 0
            )
            return (stash, final, leaving.astype(jnp.bfloat16))

        def forward_skip(state):
            return (state[0], state[1], jnp.zeros((length, width), jnp.bfloat16))

        stash, final, sending = lax.cond(active, forward_run, forward_skip, (stash, final))
        arriving = from_behind(sending, "section", 1)
        return ((arriving, stash, final), None)

    start_forward = (
        jnp.zeros((length, width), jnp.bfloat16),
        empty_kept(micro, length, width),
        jnp.zeros((micro, length, width), jnp.float32),
    )
    (unused, stash, final), unused_out = lax.scan(forward_tick, start_forward, jnp.arange(ticks))
    totals = (
        jnp.zeros((width, width + 2 * pair_width), jnp.float32),
        jnp.zeros((width, width), jnp.float32),
        jnp.zeros((width, 2 * FF), jnp.float32),
        jnp.zeros((width, FF), jnp.float32),
    )
    gains = (jnp.zeros((width,), jnp.float32), jnp.zeros((width,), jnp.float32))

    def backward_tick(carry, tick):
        arriving, gains, totals, back = carry
        micro_index = tick - (sections - 1 - section)
        active = jnp.logical_and(micro_index >= 0, micro_index < micro)
        slot = jnp.clip(micro_index, 0, micro - 1)
        given = lax.dynamic_index_in_dim(whole_cotangent, slot, 0, keepdims=False)
        incoming = jnp.where(section == sections - 1, given, arriving).astype(jnp.float32)

        def backward_run(state):
            gains, totals, back = state
            kept = jax.tree.map(
                lambda store: lax.dynamic_index_in_dim(store, slot, 0, keepdims=False), stash
            )
            kept_one = jax.tree.map(lambda item: item[0], kept)
            kept_two = jax.tree.map(lambda item: item[1], kept)
            between, terms_two, pairs_two = block_backward(incoming, kept_two, weights, tables)
            entering, terms_one, pairs_one = block_backward(between, kept_one, weights, tables)
            gains = (gains[0] + terms_one[0] + terms_two[0], gains[1] + terms_one[1] + terms_two[1])
            joined = jax.tree.map(
                lambda one, two: jnp.concatenate([one, two], axis=0), pairs_one, pairs_two
            )
            totals = jax.tree.map(jnp.add, totals, weight_parts(joined))
            back = lax.dynamic_update_index_in_dim(
                back, jnp.where(section == 0, entering, 0.0), slot, 0
            )
            return (gains, totals, back, entering.astype(jnp.bfloat16))

        def backward_skip(state):
            return (state[0], state[1], state[2], jnp.zeros((length, width), jnp.bfloat16))

        gains, totals, back, sending = lax.cond(
            active, backward_run, backward_skip, (gains, totals, back)
        )
        arriving = from_behind(sending, "section", -1)
        return ((arriving, gains, totals, back), None)

    start_backward = (
        jnp.zeros((length, width), jnp.bfloat16),
        gains,
        totals,
        jnp.zeros((micro, length, width), jnp.float32),
    )
    (unused, gains, totals, back), unused_out = lax.scan(
        backward_tick, start_backward, jnp.arange(ticks)
    )
    members = (
        gains[0].reshape(1, width, 1),
        gains[1].reshape(1, width, 1),
        totals[0][None],
        totals[1][None],
        totals[2][None],
        totals[3][None],
    )
    received = (
        lax.all_to_all(
            members[0].astype(jnp.bfloat16), "dp", split_axis=1, concat_axis=0, tiled=True
        ).astype(jnp.float32),
        lax.all_to_all(
            members[1].astype(jnp.bfloat16), "dp", split_axis=1, concat_axis=0, tiled=True
        ).astype(jnp.float32),
        lax.all_to_all(
            members[2].astype(jnp.bfloat16), "dp", split_axis=1, concat_axis=0, tiled=True
        ).astype(jnp.float32),
        lax.all_to_all(
            members[3].astype(jnp.bfloat16), "dp", split_axis=1, concat_axis=0, tiled=True
        ).astype(jnp.float32),
        lax.all_to_all(
            members[4].astype(jnp.bfloat16), "dp", split_axis=1, concat_axis=0, tiled=True
        ).astype(jnp.float32),
        lax.all_to_all(
            members[5].astype(jnp.bfloat16), "dp", split_axis=1, concat_axis=0, tiled=True
        ).astype(jnp.float32),
    )
    first_part, second_part, attend_part, branch_part, feed_part, down_part = tuple(
        (jnp.sum(item, axis=0) for item in received)
    )
    first_part = first_part[:, 0]
    second_part = second_part[:, 0]
    parts = (first_part, second_part, attend_part, branch_part, feed_part, down_part)
    squares = sum((jnp.sum(item * item) for item in parts))
    total_norm = jnp.sqrt(lax.psum(squares, ("section", "dp")))
    pieces_out, pieces_back = (
        lax.all_to_all(
            final[None].astype(jnp.bfloat16), "section", split_axis=3, concat_axis=0, tiled=True
        ).astype(jnp.float32),
        lax.all_to_all(
            back[None].astype(jnp.bfloat16), "section", split_axis=3, concat_axis=0, tiled=True
        ).astype(jnp.float32),
    )
    outputs_part = pieces_out[sections - 1]
    inputs_part = pieces_back[0]
    query_part = attend_part[:, :width]
    key_part = attend_part[:, width : width + pair_width]
    value_part = attend_part[:, width + pair_width :]
    gate_part = feed_part[:, :FF]
    up_part = feed_part[:, FF:]
    return (
        outputs_part,
        inputs_part,
        first_part[None],
        query_part[None],
        key_part[None],
        value_part[None],
        branch_part[None],
        second_part[None],
        gate_part[None],
        up_part[None],
        down_part.T[None],
        total_norm,
    )


def solution(mesh):
    return jax.shard_map(
        per_device,
        mesh=mesh,
        in_specs=(
            P("dp", None, "section"),
            P("dp", None, "section"),
            P("section", None),
            P("section", None, None),
            P("section", None, None),
            P("section", None, None),
            P("section", None, None),
            P("section", None),
            P("section", None, None),
            P("section", None, None),
            P("section", None, None),
        ),
        out_specs=(
            P("dp", None, "section"),
            P("dp", None, "section"),
            P("section", "dp"),
            P("section", "dp", None),
            P("section", "dp", None),
            P("section", "dp", None),
            P("section", "dp", None),
            P("section", "dp"),
            P("section", "dp", None),
            P("section", "dp", None),
            P("section", None, "dp"),
            P(),
        ),
        check_vma=False,
    )
```

profile of v0, /device:TPU:0, one launch (start us, length us, event | category | flops | bytes accessed | tf_op | source)
XLA Modules:
  0.0 2186.1 jit_solution(17694491218866978103)
XLA Ops:
  3.5 14.4 all_gather.7
  19.5 13.2 all_gather.6
  36.9 7.9 copy.337
  60.6 531.4 %while.70 = (s32[]{:T(128)}, bf16[32,960]{1,0:T(8,128)(2,1)S(1)}, f32[4,2,32,960]{3,2,1,0:T(8,128)}, f32[4,2,32,1]{2,1,3,0:T(2,128)}, bf16[4,2,32,960]{3,2,1,0:T...) while((s32[]{:T(128)}, bf16[32,960]{1,0:T(8,128)(2,1)S(1)}, ...), condition=%wide.region_11.12_spmd.clone.clone, body=%wide.region_0.11_spmd.clone.clone.sunk | while | flops 1271962880 | bytes 100876104 | solution.py:313
  63.5 78.0 %conditional.8 = (f32[4,2,32,960]{3,2,1,0:T(8,128)}, f32[4,2,32,1]{2,1,3,0:T(2,128)}, bf16[4,2,32,960]{3,2,1,0:T(8,128)(2,1)}, bf16[4,2,32,5,3,64]{5,4,3,2,1,0:T...) conditional(s32[]{:T(128)} %convert_element_type.482, ...), branch_computations={%region_1.1_spmd, %region_2.10_spmd} | conditional | flops 1271901440 | bytes 100375600 | solution.py:304
  147.8 78.1 %conditional.8 = (f32[4,2,32,960]{3,2,1,0:T(8,128)}, f32[4,2,32,1]{2,1,3,0:T(2,128)}, bf16[4,2,32,960]{3,2,1,0:T(8,128)(2,1)}, bf16[4,2,32,5,3,64]{5,4,3,2,1,0:T...) conditional(s32[]{:T(128)} %convert_element_type.482, ...), branch_computations={%region_1.1_spmd, %region_2.10_spmd} | conditional | flops 1271901440 | bytes 100375600 | solution.py:304
  235.0 78.0 %conditional.8 = (f32[4,2,32,960]{3,2,1,0:T(8,128)}, f32[4,2,32,1]{2,1,3,0:T(2,128)}, bf16[4,2,32,960]{3,2,1,0:T(8,128)(2,1)}, bf16[4,2,32,5,3,64]{5,4,3,2,1,0:T...) conditional(s32[]{:T(128)} %convert_element_type.482, ...), branch_computations={%region_1.1_spmd, %region_2.10_spmd} | conditional | flops 1271901440 | bytes 100375600 | solution.py:304
  322.2 78.0 %conditional.8 = (f32[4,2,32,960]{3,2,1,0:T(8,128)}, f32[4,2,32,1]{2,1,3,0:T(2,128)}, bf16[4,2,32,960]{3,2,1,0:T(8,128)(2,1)}, bf16[4,2,32,5,3,64]{5,4,3,2,1,0:T...) conditional(s32[]{:T(128)} %convert_element_type.482, ...), branch_computations={%region_1.1_spmd, %region_2.10_spmd} | conditional | flops 1271901440 | bytes 100375600 | solution.py:304
  410.0 81.5 %collective-permute-start = (bf16[32,960]{1,0:T(8,128)(2,1)}, bf16[32,960]{1,0:T(8,128)(2,1)S(1)}, u32[]{:S(2)}, u32[]{:S(2)}) collective-permute-start(bf16[32,960]{1,0:T(8,128)(2,1)} %get-tuple-element.2450), channel_id=1, source_target_pairs={{0,8},{8,16},{16,24},{1,9},{9,17},{17,25},{2,10},{10,18},{18,26},{... | collective-permute-start | bytes 184328 | tf_op jit(solution)/shard_map/while/body/eval_jaxpr/ppermute | solution.py:19
  507.5 82.3 %collective-permute-start = (bf16[32,960]{1,0:T(8,128)(2,1)}, bf16[32,960]{1,0:T(8,128)(2,1)S(1)}, u32[]{:S(2)}, u32[]{:S(2)}) collective-permute-start(bf16[32,960]{1,0:T(8,128)(2,1)} %get-tuple-element.2450), channel_id=1, source_target_pairs={{0,8},{8,16},{16,24},{1,9},{9,17},{17,25},{2,10},{10,18},{18,26},{... | collective-permute-start | bytes 184328 | tf_op jit(solution)/shard_map/while/body/eval_jaxpr/ppermute | solution.py:19
  609.8 9.1 broadcast_in_dim.159
  618.8 916.8 %while.71 = (s32[]{:T(128)}, bf16[32,960]{1,0:T(8,128)(2,1)S(1)}, f32[960]{0:T(1024)S(1)}, f32[960]{0:T(1024)S(1)}, f32[960,1600]{1,0:T(8,128)}, /*index=5*/f32[...) while((s32[]{:T(128)}, bf16[32,960]{1,0:T(8,128)(2,1)S(1)}, ...), condition=%wide.region_25.26_spmd.clone.clone, body=%wide.region_12.25_spmd.clone.clone.sunk | while | flops 2556162048 | bytes 296641568 | solution.py:364
  634.9 79.5 %collective-permute-done.1 = bf16[32,960]{1,0:T(8,128)(2,1)S(1)} collective-permute-done((bf16[32,960]{1,0:T(8,128)(2,1)}, bf16[32,960]{1,0:T(8,128)(2,1)S(1)}, u32[]{:S(2)}, u32[]{:S(2)}) %collective-permute-start.1) | collective-permute-done | bytes 61472 | tf_op jit(solution)/shard_map/while/body/eval_jaxpr/ppermute | solution.py:19
  719.1 334.7 %collective-permute-done.1 = bf16[32,960]{1,0:T(8,128)(2,1)S(1)} collective-permute-done((bf16[32,960]{1,0:T(8,128)(2,1)}, bf16[32,960]{1,0:T(8,128)(2,1)S(1)}, u32[]{:S(2)}, u32[]{:S(2)}) %collective-permute-start.1) | collective-permute-done | bytes 61472 | tf_op jit(solution)/shard_map/while/body/eval_jaxpr/ppermute | solution.py:19
  1056.6 110.6 %conditional.9 = (f32[960]{0:T(1024)S(1)}, f32[960]{0:T(1024)S(1)}, f32[960,1600]{1,0:T(8,128)}, f32[960,960]{1,0:T(8,128)}, f32[960,5120]{1,0:T(8,128)}, /*inde...) conditional(s32[]{:T(128)} %convert_element_type.484, (f32[960]{0:T(1024)S(1)}, ...), branch_computations={%region_13.13_spmd, %region_14.24_spmd} | conditional | flops 2556100608 | bytes 296141024 | solution.py:352
  1142.8 6.6 convolution_add_fusion.6
  1151.4 15.7 convolution_add_fusion.4
  1177.3 110.6 %conditional.9 = (f32[960]{0:T(1024)S(1)}, f32[960]{0:T(1024)S(1)}, f32[960,1600]{1,0:T(8,128)}, f32[960,960]{1,0:T(8,128)}, f32[960,5120]{1,0:T(8,128)}, /*inde...) conditional(s32[]{:T(128)} %convert_element_type.484, (f32[960]{0:T(1024)S(1)}, ...), branch_computations={%region_13.13_spmd, %region_14.24_spmd} | conditional | flops 2556100608 | bytes 296141024 | solution.py:352
  1263.5 6.6 convolution_add_fusion.6
  1272.2 15.7 convolution_add_fusion.4
  1297.9 110.6 %conditional.9 = (f32[960]{0:T(1024)S(1)}, f32[960]{0:T(1024)S(1)}, f32[960,1600]{1,0:T(8,128)}, f32[960,960]{1,0:T(8,128)}, f32[960,5120]{1,0:T(8,128)}, /*inde...) conditional(s32[]{:T(128)} %convert_element_type.484, (f32[960]{0:T(1024)S(1)}, ...), branch_computations={%region_13.13_spmd, %region_14.24_spmd} | conditional | flops 2556100608 | bytes 296141024 | solution.py:352
  1384.0 6.6 convolution_add_fusion.6
  1392.7 15.7 convolution_add_fusion.4
  1418.5 110.6 %conditional.9 = (f32[960]{0:T(1024)S(1)}, f32[960]{0:T(1024)S(1)}, f32[960,1600]{1,0:T(8,128)}, f32[960,960]{1,0:T(8,128)}, f32[960,5120]{1,0:T(8,128)}, /*inde...) conditional(s32[]{:T(128)} %convert_element_type.484, (f32[960]{0:T(1024)S(1)}, ...), branch_computations={%region_13.13_spmd, %region_14.24_spmd} | conditional | flops 2556100608 | bytes 296141024 | solution.py:352
  1504.7 6.6 convolution_add_fusion.6
  1513.4 15.7 convolution_add_fusion.4
  1550.9 8.2 all-to-all-done.5
  1566.4 11.6 all-to-all-done.2
  1597.9 12.5 reduce.9
  1623.2 19.6 copy.439
  1642.8 19.8 reduce.8
  1662.6 7.5 reshape.741
  1679.9 27.9 %copy.438 = bf16[1,960,2560]{2,0,1:T(2,128)(2,1)} copy(bf16[1,960,2560]{2,1,0:T(8,128)(2,1)S(1)} %convert_bitcast_fusion.1) | data formatting | bytes 9830400 | tf_op jit(solution)/shard_map/convert_element_type | solution.py:392
  1707.8 31.2 %reduce.11 = bf16[960,2560]{1,0:T(8,128)(2,1)} reduce(bf16[960,1,2560]{2,1,0:T(2,128)(2,1)} %bitcast.519, bf16[]{:T(256)} %broadcast.368), dimensions={1}, to_apply=%bitcast.470.reduce_sub_computation | reduce | bytes 9830402
  1739.0 7.7 reshape.747
  1751.8 7.6 convert_bitcast_fusion
  1759.4 48.8 %copy.437 = bf16[1,960,5120]{2,0,1:T(2,128)(2,1)} copy(bf16[1,960,5120]{2,1,0:T(8,128)(2,1)S(1)} %convert_bitcast_fusion) | data formatting | bytes 19660800 | tf_op jit(solution)/shard_map/convert_element_type | solution.py:389
  1808.2 59.6 %reduce.10 = bf16[960,5120]{1,0:T(8,128)(2,1)} reduce(bf16[960,1,5120]{2,1,0:T(2,128)(2,1)} %bitcast.504, bf16[]{:T(256)} %broadcast.368), dimensions={1}, to_apply=%bitcast.469.reduce_sub_computation | reduce | bytes 19660802
  1867.8 11.7 reshape.745
  1903.3 7.9 reshape.744
  1921.3 8.5 reshape.742
  1943.5 9.6 reshape.748
  1953.1 8.4 copy.396
  1967.2 132.5 %all-to-all-done.6 = bf16[8,2,307200]{2,1,0:T(2,128)(2,1)} async-done(((bf16[8,2,307200]{2,1,0:T(2,128)(2,1)}), bf16[8,2,307200]{2,1,0:T(2,128)(2,1)}, u32[]{:S(2)}, u32[]{:S(2)}) %all-to-all-start.6) | async-done | bytes 9830432 | tf_op jit(solution)/shard_map/all_to_all | solution.py:388
  2099.7 14.9 reshape.746
  2114.6 18.5 copy.395
  2133.1 8.6 reduce_sum.256
  2145.8 38.2 %psum.7 = f32[]{:T(128)} all-reduce(f32[]{:T(128)S(6)} %add.317), channel_id=1, replica_groups=mesh['section'=4,'dp'=8] {'section','dp'}, use_global_device_ids=true, to_apply=%region_38.39 | all-reduce | flops 1 | bytes 8 | tf_op jit(solution)/shard_map/psum | solution.py:402
  (1522 shorter events, 934.1 us)
Async XLA Ops:
  0.6 33.7 %copy-start.61 = (bf16[1,960,320]{1,2,0:T(8,128)(2,1)S(1)}, bf16[1,960,320]{1,2,0:T(8,128)(2,1)}, u32[]{:S(2)}) copy-start(bf16[1,960,320]{1,2,0:T(8,128)(2,1)} %param.23) | copy-start | bytes 1843204
  64.2 17.0 copy-start.59
  141.6 3.5 collective-permute-start
  148.5 17.0 copy-start.59
  225.9 6.3 collective-permute-start
  235.7 17.0 copy-start.59
  313.0 6.4 collective-permute-start
  322.8 17.0 copy-start.59
  400.2 6.4 collective-permute-start
  410.0 84.2 %collective-permute-start = (bf16[32,960]{1,0:T(8,128)(2,1)}, bf16[32,960]{1,0:T(8,128)(2,1)S(1)}, u32[]{:S(2)}, u32[]{:S(2)}) collective-permute-start(bf16[32,960]{1,0:T(8,128)(2,1)} %get-tuple-element.2450), channel_id=1, source_target_pairs={{0,8},{8,16},{16,24},{1,9},{9,17},{17,25},{2,10},{10,18},{18,26},{... | collective-permute-start | bytes 184328 | tf_op jit(solution)/shard_map/while/body/eval_jaxpr/ppermute | solution.py:19
  497.6 6.5 collective-permute-start
  507.5 84.5 %collective-permute-start = (bf16[32,960]{1,0:T(8,128)(2,1)}, bf16[32,960]{1,0:T(8,128)(2,1)S(1)}, u32[]{:S(2)}, u32[]{:S(2)}) collective-permute-start(bf16[32,960]{1,0:T(8,128)(2,1)} %get-tuple-element.2450), channel_id=1, source_target_pairs={{0,8},{8,16},{16,24},{1,9},{9,17},{17,25},{2,10},{10,18},{18,26},{... | collective-permute-start | bytes 184328 | tf_op jit(solution)/shard_map/while/body/eval_jaxpr/ppermute | solution.py:19
  622.7 7.5 collective-permute-start.1
  633.6 80.8 %collective-permute-start.1 = (bf16[32,960]{1,0:T(8,128)(2,1)}, bf16[32,960]{1,0:T(8,128)(2,1)S(1)}, u32[]{:S(2)}, u32[]{:S(2)}) collective-permute-start(bf16[32,960]{1,0:T(8,128)(2,1)} %get-tuple-element.2505), channel_id=1, source_target_pairs={{8,0},{16,8},{24,16},{9,1},{17,9},{25,17},{10,2},{18,10},{26,18},{... | collective-permute-start | bytes 184328 | tf_op jit(solution)/shard_map/while/body/eval_jaxpr/ppermute | solution.py:19
  717.8 335.9 %collective-permute-start.1 = (bf16[32,960]{1,0:T(8,128)(2,1)}, bf16[32,960]{1,0:T(8,128)(2,1)S(1)}, u32[]{:S(2)}, u32[]{:S(2)}) collective-permute-start(bf16[32,960]{1,0:T(8,128)(2,1)} %get-tuple-element.2505), channel_id=1, source_target_pairs={{8,0},{16,8},{24,16},{9,1},{17,9},{25,17},{10,2},{18,10},{26,18},{... | collective-permute-start | bytes 184328 | tf_op jit(solution)/shard_map/while/body/eval_jaxpr/ppermute | solution.py:19
  1090.0 21.4 slice-start.4
  1151.4 15.8 copy-start.4
  1151.4 15.8 copy-start.65
  1151.4 15.8 copy-start.67
  1167.2 7.3 collective-permute-start.1
  1210.7 21.4 slice-start.4
  1272.1 15.8 copy-start.4
  1272.1 15.8 copy-start.65
  1272.2 15.8 copy-start.67
  1287.9 7.2 collective-permute-start.1
  1331.3 21.4 slice-start.4
  1392.7 15.8 copy-start.4
  1392.7 15.8 copy-start.65
  1392.7 15.8 copy-start.67
  1408.5 7.3 collective-permute-start.1
  1451.9 21.4 slice-start.4
  1513.3 15.8 copy-start.4
  1513.3 15.8 copy-start.65
  1513.3 15.8 copy-start.67
  1529.1 6.4 collective-permute-start.1
  1535.7 29.7 %copy-start.56 = (bf16[4,32,960]{2,1,0:T(8,128)(2,1)S(1)}, bf16[4,32,960]{2,1,0:T(8,128)(2,1)}, u32[]{:S(2)}) copy-start(bf16[4,32,960]{2,1,0:T(8,128)(2,1)} %get-tuple-element.992) | copy-start | bytes 737284
  1539.6 19.5 all-to-all-start.5
  1559.9 18.1 all-to-all-start.2
  1578.0 14.5 copy-start.55
  1578.0 8.7 all-to-all-start
  1586.7 29.0 %all-to-all-start.1 = ((bf16[4,2,15360]{2,1,0:T(2,128)(2,1)}), bf16[4,2,15360]{2,1,0:T(2,128)(2,1)S(1)}, u32[]{:S(2)}, u32[]{:S(2)}) async-start(bf16[4,2,15360]{2,1,0:T(2,128)(2,1)} %reshape.751), calls=%async_computation.1 | async-start | bytes 491520 | tf_op jit(solution)/shard_map/all_to_all | solution.py:407
  1615.7 54.4 %all-to-all-start.4 = ((bf16[8,2,57600]{2,1,0:T(2,128)(2,1)}), bf16[8,2,57600]{2,1,0:T(2,128)(2,1)}, u32[]{:S(2)}, u32[]{:S(2)}) async-start(bf16[8,2,57600]{2,1,0:T(2,128)(2,1)} %reshape.743), calls=%async_computation.4 | async-start | bytes 3686400 | tf_op jit(solution)/shard_map/all_to_all | solution.py:385
  1670.1 76.6 %all-to-all-start.3 = ((bf16[8,2,96000]{2,1,0:T(2,128)(2,1)}), bf16[8,2,96000]{2,1,0:T(2,128)(2,1)S(1)}, u32[]{:S(2)}, u32[]{:S(2)}) async-start(bf16[8,2,96000]{2,1,0:T(2,128)(2,1)} %reshape.741), calls=%async_computation.3 | async-start | bytes 6144000 | tf_op jit(solution)/shard_map/all_to_all | solution.py:382
  1746.7 132.9 %all-to-all-start.7 = ((bf16[8,2,153600]{2,1,0:T(2,128)(2,1)}), bf16[8,2,153600]{2,1,0:T(2,128)(2,1)}, u32[]{:S(2)}, u32[]{:S(2)}) async-start(bf16[8,2,153600]{2,1,0:T(2,128)(2,1)} %reshape.747), calls=%async_computation.7 | async-start | bytes 9830400 | tf_op jit(solution)/shard_map/all_to_all | solution.py:391
  1879.6 220.2 %all-to-all-start.6 = ((bf16[8,2,307200]{2,1,0:T(2,128)(2,1)}), bf16[8,2,307200]{2,1,0:T(2,128)(2,1)}, u32[]{:S(2)}, u32[]{:S(2)}) async-start(bf16[8,2,307200]{2,1,0:T(2,128)(2,1)} %reshape.745), calls=%async_computation.6 | async-start | bytes 19660800 | tf_op jit(solution)/shard_map/all_to_all | solution.py:388
  1891.2 20.0 copy-start.73
  1891.3 19.9 copy-start.74
  1966.3 148.3 %copy-start.52 = (f32[120,2560]{1,0:T(8,128)}, f32[120,2560]{1,0:T(8,128)S(1)}, u32[]{:S(2)}) copy-start(f32[120,2560]{1,0:T(8,128)S(1)} %reduce_sum.257) | copy-start | bytes 3686404
  (296 other events, 1629.9 us)
where the time goes:
time: 2200 us; the launch traced here: 2190 us
  waiting for transfers between devices  615 us (28%)
  local copies, waits for them, and re-layouts  508 us (23%)
  matrix products  382 us (17%)
  other arithmetic  367 us (17%)
  starting transfers between devices  226 us (10%)
  blocking collectives  65.8 us (3%)
    ppermute x14, waiting for transfers between devices, from_behind(): return lax.ppermute(block, axis, route)  459 us
    ppermute x14, starting transfers between devices, from_behind(): return lax.ppermute(block, axis, route)  191 us
    unnamed x54, local copies, waits for them, and re-layouts  147 us
    all_to_all x1, waiting for transfers between devices, per_device(): lax.all_to_all(members[4].astype(jnp.bfloat16), 'dp', split_axis=1, conca...  132 us
    unnamed x4, other arithmetic  123 us
    dot_general x16, matrix products, outer_sum(): lax.dot_general(left, right, (((0,), (0,)), ((), ())), preferred_element_...  117 us
    dot_general x56, matrix products, transposed(): lax.dot_general(left, right, (((1,), (1,)), ((), ())), preferred_element_...  110 us
    dot_general x56, matrix products, matmul(): return jnp.dot(left, right, preferred_element_type=jnp.float32)  99.6 us
  transfers between devices with their start and end apart: 22, of which 18 were waited for; matrix products, arithmetic and copies ran while one was open for 17% of the time, Pallas kernels for 0%

commit v1 on v0

v1 whole, which is shorter than its diff:
```python
import functools

import jax
import jax.numpy as jnp
import numpy as np
from jax import lax
from jax.experimental import pallas as pl
from jax.experimental.pallas import tpu as pltpu
from jax.sharding import PartitionSpec as P

HEADS = 15
KV_HEADS = 5
HEAD = 64
EPSILON = 1e-05
THETA = 10000.0
LANES = 128
PIECES = 2
BAND = 1024
BF = jnp.bfloat16
F32 = jnp.float32
QUERY = HEADS * HEAD
PAIR = KV_HEADS * HEAD
JOINED = QUERY + 2 * PAIR + HEAD
CHUNKS = (HEADS + 1) // 2
MEGA = 2**20


def dot(left, right):
    return jnp.dot(left, right, preferred_element_type=F32)


def dot_last(left, right):
    return lax.dot_general(left, right, (((1,), (1,)), ((), ())), preferred_element_type=F32)


def dot_first(left, right):
    return lax.dot_general(left, right, (((0,), (0,)), ((), ())), preferred_element_type=F32)


def rotary_tables(length, rows):
    half = HEAD // 2
    frequency = THETA ** (-(np.arange(half, dtype=np.float64) * 2.0 / HEAD))
    angles = np.arange(length, dtype=np.float64)[:, None] * frequency[None, :]
    angles = np.concatenate([angles] * (LANES // half), axis=-1)
    sign = np.where(np.arange(LANES) % HEAD < half, -1.0, 1.0)
    copies = (rows // length, 1)
    return (
        np.tile(np.cos(angles), copies).astype(np.float32),
        np.tile(np.sin(angles) * sign, copies).astype(np.float32),
    )


def lane_index(rows):
    return lax.broadcasted_iota(jnp.int32, (rows, LANES), 1)


def half_turned(chunk, first_half):
    return jnp.where(first_half, pltpu.roll(chunk, LANES - HEAD // 2, 1), pltpu.roll(chunk, HEAD // 2, 1))


def mean_scale(residual):
    return lax.rsqrt(jnp.mean(residual * residual, axis=-1, keepdims=True) + EPSILON)


def group_of(head):
    return head // (HEADS // KV_HEADS)


def chunk_heads(chunk):
    return [head for head in (2 * chunk, 2 * chunk + 1) if head < HEADS]


def spread_groups(chunks, first_lane, lower):
    low, high = {}, {}
    for group in range(KV_HEADS):
        column = first_lane + group * HEAD
        chunk = chunks[column // LANES]
        swapped = pltpu.roll(chunk, HEAD, 1)
        here, there = (chunk, swapped) if column % LANES == 0 else (swapped, chunk)
        low[group] = jnp.where(lower, here, 0.0).astype(BF)
        high[group] = jnp.where(lower, 0.0, there).astype(BF)
    return low, high


def chunk_operand(spread, chunk):
    return [spread[head % 2][group_of(head)] for head in chunk_heads(chunk)]


LEFTS = ("normed", "context", "second")


def wide_views(wide, width):
    return [wide.at[pl.ds(i * width, width)] for i in range(3)]


def tall_views(tall, hidden, width):
    return [tall.at[pl.ds(i * hidden, size)] for i, size in enumerate((hidden, hidden, hidden, width))]


def stash_widths(hidden):
    return {
        "query": CHUNKS * LANES,
        "keys": KV_HEADS * 2 * LANES,
        "values": KV_HEADS * 2 * LANES,
        "chances": CHUNKS * 2 * LANES,
        "gate_factor": hidden,
        "up_factor": hidden,
    }


def stash_shape(rows, hidden):
    return (2, rows, sum(stash_widths(hidden).values()))


def views(ref, widths, app):
    starts, start = {}, 0
    for name, width in widths.items():
        starts[name] = start
        start += -(-width // LANES) * LANES

    def get(name, low=0, high=None):
        high = widths[name] if high is None else high
        return ref[app, :, starts[name] + low : starts[name] + high]

    def put(name, value, low=0):
        ref[app, :, starts[name] + low : starts[name] + low + value.shape[1]] = value

    return get, put


def assembled(pieces):
    return jnp.concatenate([piece[...] for piece in pieces], axis=1)


def forward_kernel(tick, rows, length, hidden, old, count, section, gain_one, gain_two, cosine, sine, *rest):
    x, rest = rest[:count], rest[count:]
    (wide, tall, vqkv), (result, leaving), rest = rest[:3], rest[3 + old : 5 + old], rest[8 + old :]
    stash, sums, *left_out, left, left_sems = rest
    width = result.shape[1]
    vg, vu, _ = wide_views(wide, width)
    vd, _, _, vo = tall_views(tall, hidden, width)
    piece = hidden // PIECES

    @pl.when(section[0] == tick)
    def run():
        lanes = lane_index(rows)
        lower = lanes < HEAD
        first_half = lax.rem(lanes, HEAD) < HEAD // 2
        token = lax.broadcasted_iota(jnp.int32, (rows, rows), 0)
        other = lax.broadcasted_iota(jnp.int32, (rows, rows), 1)
        seen = jnp.logical_and(token <= other, lax.div(other, length) == lax.div(token, length))
        cos, sin = cosine[...], sine[...]
        residual = assembled(x).astype(F32)
        writes = []
        for app in range(2):
            def give(name, value, app=app):
                i = LEFTS.index(name)
                left[i, app] = value
                write = pltpu.make_async_copy(left.at[i, app], left_out[i].at[app], left_sems.at[i, app])
                write.start()
                writes.append(write)

            get, put = views(stash, stash_widths(hidden), app)
            sums[0, app] = residual
            normed = (residual * mean_scale(residual) * gain_one[...]).astype(BF)
            give("normed", normed)
            joined = dot(normed, vqkv[...])
            chunks = [joined[:, i * LANES : (i + 1) * LANES] for i in range(JOINED // LANES)]
            turned = (QUERY + PAIR) // LANES
            for i in range(turned):
                chunks[i] = chunks[i] * cos + half_turned(chunks[i], first_half) * sin
            queries = [chunk.astype(BF) for chunk in chunks[:CHUNKS]]
            keys = spread_groups(chunks, QUERY, lower)
            values = spread_groups(chunks, QUERY + PAIR, lower)
            for name, (low, high) in (("keys", keys), ("values", values)):
                for group in range(KV_HEADS):
                    at = 2 * group * LANES
                    put(name, low[group], at)
                    put(name, high[group], at + LANES)
            contexts = []
            for c in range(CHUNKS):
                put("query", queries[c], c * LANES)
                key_side, value_side = chunk_operand(keys, c), chunk_operand(values, c)
                if len(key_side) == 1:
                    key_side = key_side + [jnp.zeros_like(key_side[0])]
                    value_side = value_side + [jnp.zeros_like(value_side[0])]
                parts = []
                for side in range(2):
                    at = (2 * c + side) * LANES
                    if 2 * c + side >= HEADS:
                        parts.append(jnp.zeros((rows, rows), BF))
                        continue
                    scores = dot_last(key_side[side], queries[c]) * HEAD ** (-0.5)
                    scores = jnp.where(seen, scores, -1e30)
                    highest = jnp.max(scores, axis=0, keepdims=True)
                    powers = jnp.exp(scores - highest)
                    total = jnp.sum(powers, axis=0, keepdims=True)
                    parts.append((powers * (1.0 / total)).astype(BF))
                    put("chances", parts[side], at)
                contexts.append(dot_first(jnp.concatenate(parts, axis=0), jnp.concatenate(value_side, axis=0)).astype(BF))
            context = jnp.concatenate(contexts, axis=1)[:, :QUERY]
            give("context", context)
            middle = residual + dot(context, vo[...])
            sums[1, app] = middle
            second = (middle * mean_scale(middle) * gain_two[...]).astype(BF)
            give("second", second)
            total = middle
            for i in range(PIECES):
                cols = slice(i * piece, (i + 1) * piece)
                gate = dot(second, vg[:, cols])
                up = dot(second, vu[:, cols])
                sigma = jax.nn.sigmoid(gate)
                linear = gate * sigma
                put("gate_factor", (up * (sigma + linear * (1.0 - sigma))).astype(BF), i * piece)
                put("up_factor", linear.astype(BF), i * piece)
                total = total + dot((linear * up).astype(BF), vd[cols])
            residual = total
        result[...] = residual
        leaving[...] = residual.astype(BF)
        for write in writes:
            write.wait()


def vmem():
    return pl.BlockSpec(memory_space=pltpu.VMEM)


def anywhere():
    return pl.BlockSpec(memory_space=pl.ANY)


def pinned(arrays):
    return [pltpu.with_memory_space_constraint(array, pltpu.HBM) for array in arrays]


def resident(arrays):
    return [pltpu.with_memory_space_constraint(array, pltpu.VMEM) for array in arrays]


def vmem_like(arrays):
    return [pltpu.VMEM(array.shape, array.dtype) for array in arrays]


def forward_pass(tick, section, x, gains, tables, weights, stash, lefts, length, hidden):
    rows, width = x[0].shape[0], weights[1].shape[1]
    held = [*weights, *stash]
    count = len(x)
    outs = pl.pallas_call(
        functools.partial(forward_kernel, tick, rows, length, hidden, len(stash) + len(lefts), count),
        out_shape=[
            jax.ShapeDtypeStruct((rows, width), F32),
            jax.ShapeDtypeStruct((rows, width), BF),
        ]
        + vmem_like(weights)
        + [pltpu.VMEM(stash_shape(rows, hidden), BF), pltpu.VMEM((2, 2, rows, width), F32)]
        + [pltpu.HBM((2, rows, width), BF)] * len(LEFTS),
        in_specs=[pl.BlockSpec(memory_space=pltpu.SMEM)]
        + [vmem()] * (4 + count + len(held))
        + [pl.BlockSpec(memory_space=pltpu.HBM)] * len(lefts),
        out_specs=[vmem()] * 7 + [pl.BlockSpec(memory_space=pltpu.HBM)] * len(LEFTS),
        scratch_shapes=[
            pltpu.VMEM((len(LEFTS), 2, rows, width), BF),
            pltpu.SemaphoreType.DMA((len(LEFTS), 2)),
        ],
        input_output_aliases={5 + count + i: 2 + i for i in range(len(held) + len(lefts))},
        compiler_params=pltpu.CompilerParams(vmem_limit_bytes=16 * MEGA),
        name="forward_pass",
    )(section, *resident((*gains, *tables, *x, *held)), *pinned(lefts))
    return outs[0], outs[1], outs[2:5], outs[5:7], outs[7:]


SLOPES = {"branch": QUERY, "attend": JOINED, "first": QUERY, "second": QUERY}
SLOPES_WIDTH = sum(-(-width // LANES) * LANES for width in SLOPES.values())


def backward_kernel(tick, rows, length, hidden, old, count, section, gain_one, gain_two, cosine, sine, *rest):
    slope_in, rest = rest[:count], rest[count:]
    (wot, wqkvt, wide, tall, stash, sums), rest = rest[:6], rest[6 + old :]
    entering, leaving, _, _, _, _, made, mixer_out, vot, vqkvt, mixers, sems, mixer_sems = rest
    width = entering.shape[1]
    _, _, vdt = wide_views(wide, width)
    _, vgt, vut, _ = tall_views(tall, hidden, width)
    piece = hidden // PIECES

    @pl.when(section[0] == tick)
    def run():
        lanes = lane_index(rows)
        lower = lanes < HEAD
        first_half = lax.rem(lanes, HEAD) < HEAD // 2
        cos, sin = cosine[...], sine[...]
        copies = [
            pltpu.make_async_copy(wot, vot, sems.at[0]),
            pltpu.make_async_copy(wqkvt, vqkvt, sems.at[1]),
        ]
        for copy in copies:
            copy.start()
        slope = assembled(slope_in).astype(F32)
        writes = []
        for app in (1, 0):
            get, _ = views(stash, stash_widths(hidden), app)
            _, put = views(made, SLOPES, app)
            mixer = slope.astype(BF)
            mixers[app] = mixer
            writes.append(pltpu.make_async_copy(mixers.at[app], mixer_out.at[app], mixer_sems.at[app]))
            writes[-1].start()
            back = None
            for i in range(PIECES):
                cols = slice(i * piece, (i + 1) * piece)
                active = dot(mixer, vdt[:, cols])
                gate = (active * get("gate_factor", i * piece, (i + 1) * piece).astype(F32)).astype(BF)
                up = (active * get("up_factor", i * piece, (i + 1) * piece).astype(F32)).astype(BF)
                part = dot(gate, vgt[cols]) + dot(up, vut[cols])
                back = part if back is None else back + part
            middle = sums[1, app]
            scale = mean_scale(middle)
            shaped = back * gain_two[...]
            inner = jnp.mean(shaped * middle, axis=-1, keepdims=True)
            put("second", (back * middle * scale).astype(BF))
            middle_slope = slope + scale * shaped - middle * (scale * scale * scale * inner)
            branch = middle_slope.astype(BF)
            put("branch", branch)
            if app == 1:
                copies[0].wait()
            context_slope = dot(branch, vot[...])
            query_back, key_back, value_back = [], {}, {}
            for c in range(CHUNKS):
                here = slice(c * LANES, (c + 1) * LANES)
                piece_slope = context_slope[:, here]
                rounded = piece_slope.astype(BF)
                sides = range(len(chunk_heads(c)))

                def operand(name):
                    places = [
                        2 * c + side if name == "chances" else 2 * group_of(2 * c + side) + side for side in sides
                    ]
                    return jnp.concatenate(
                        [get(name, place * LANES, (place + 1) * LANES) for place in places], axis=0
                    )

                chances = operand("chances")
                slopes_here = dot_last(operand("values"), rounded)
                scores = []
                for side in sides:
                    band = slice(side * rows, (side + 1) * rows)
                    chance, chance_slope = chances[band].astype(F32), slopes_here[band]
                    inner = jnp.sum(chance * chance_slope, axis=0, keepdims=True)
                    scores.append((chance * (chance_slope - inner)).astype(BF))
                score = jnp.concatenate(scores, axis=0)
                query_back.append(dot_first(score, operand("keys")))
                key_part = dot(score, get("query", c * LANES, (c + 1) * LANES))
                value_part = dot(chances, rounded)
                for head in chunk_heads(c):
                    side, group = head % 2, group_of(head)
                    band = slice(side * rows, (side + 1) * rows)
                    for store, part in ((key_back, key_part), (value_back, value_part)):
                        item = part[band]
                        store[group, side] = store[group, side] + item if (group, side) in store else item

            def gathered(store, group, up_half):
                low, high = store[group, 0], store[group, 1]
                if up_half:
                    return pltpu.roll(low, HEAD, 1) + high
                return low + pltpu.roll(high, HEAD, 1)

            chunks = query_back + [None] * (JOINED // LANES - CHUNKS)
            for store, start in ((key_back, QUERY), (value_back, QUERY + PAIR)):
                for group in range(KV_HEADS):
                    at, offset = divmod(start + group * HEAD, LANES)
                    item = gathered(store, group, offset > 0)
                    if offset == 0:
                        chunks[at] = jnp.where(lower, item, 0.0)
                    else:
                        chunks[at] = jnp.where(lower, chunks[at], item)
            for i in range((QUERY + PAIR) // LANES):
                chunks[i] = (chunks[i] * cos - half_turned(chunks[i], first_half) * sin) * HEAD ** (-0.5)
            attend = jnp.concatenate([chunk.astype(BF) for chunk in chunks], axis=1)
            put("attend", attend)
            if app == 1:
                copies[1].wait()
            back = dot(attend, vqkvt[...])
            residual = sums[0, app]
            scale = mean_scale(residual)
            shaped = back * gain_one[...]
            inner = jnp.mean(shaped * residual, axis=-1, keepdims=True)
            put("first", (back * residual * scale).astype(BF))
            slope = middle_slope + scale * shaped - residual * (scale * scale * scale * inner)
        entering[...] = slope
        leaving[...] = slope.astype(BF)
        for write in writes:
            write.wait()


def backward_pass(tick, section, slope, gains, tables, stash, streamed, weights, made, mixers, length, hidden, behind):
    rows, width = slope[0].shape[0], weights[1].shape[1]
    held = [*weights, *stash, *made]
    count = len(slope)
    outs = pl.pallas_call(
        functools.partial(backward_kernel, tick, rows, length, hidden, len(made) + len(mixers) + len(behind), count),
        out_shape=[
            jax.ShapeDtypeStruct((rows, width), F32),
            jax.ShapeDtypeStruct((rows, width), BF),
        ]
        + vmem_like([*weights, *stash])
        + [pltpu.VMEM((2, rows, SLOPES_WIDTH), BF), pltpu.HBM((2, rows, width), BF)],
        in_specs=[pl.BlockSpec(memory_space=pltpu.SMEM)]
        + [vmem()] * (4 + count)
        + [pl.BlockSpec(memory_space=pltpu.HBM)] * 2
        + [vmem()] * len(held)
        + [pl.BlockSpec(memory_space=pltpu.HBM)] * len(mixers)
        + [pl.BlockSpec(memory_space=pl.ANY)] * len(behind),
        out_specs=[vmem()] * 7 + [pl.BlockSpec(memory_space=pltpu.HBM)],
        scratch_shapes=[pltpu.VMEM(w.shape, BF) for w in streamed]
        + [pltpu.VMEM((2, rows, width), BF)]
        + [pltpu.SemaphoreType.DMA((2,))] * 2,
        input_output_aliases={7 + count + i: 2 + i for i in range(len(held) + len(mixers))},
        compiler_params=pltpu.CompilerParams(vmem_limit_bytes=16 * MEGA),
        name="backward_pass",
    )(section, *resident((*gains, *tables, *slope)), *pinned(streamed), *resident(held), *pinned(mixers), *behind)
    return outs[0], outs[1], outs[2:4], outs[4:6], outs[6:7], outs[7:]


def turn(source, target, row=0, column=0):
    depth, width = source.shape
    for start in range(0, width, LANES):
        stop = min(start + LANES, width)
        target[row + start : row + stop, column : column + depth] = source[:, start:stop].T


def load_kernel(wq, wkt, wvt, wo, wg, wu, wdt, wide, tall, vqkv, wqkvt, sq, vqkvt, sems, out_sem):
    width, pair = wq.shape[0], wkt.shape[0]
    vg, vu, vdt = wide_views(wide, width)
    vd, _, _, vo = tall_views(tall, wg.shape[1], width)
    copies = [
        pltpu.make_async_copy(source, target, sems.at[i])
        for i, (source, target) in enumerate(
            (
                (wq, sq),
                (wkt, vqkvt.at[pl.ds(width, pair)]),
                (wvt, vqkvt.at[pl.ds(width + pair, pair)]),
                (wdt, vdt),
                (wo, vo),
                (wg, vg),
                (wu, vu),
            )
        )
    ]
    for copy in copies:
        copy.start()
    vqkvt[width + 2 * pair :] = jnp.zeros((HEAD, width), BF)
    for copy in copies[:3]:
        copy.wait()
    vqkv[:, :width] = sq[...]
    vqkv[:, width:] = vqkvt[width:, :].T
    turn(sq, vqkvt)
    out = pltpu.make_async_copy(vqkvt, wqkvt, out_sem)
    out.start()
    copies[3].wait()
    turn(vdt, vd)
    for copy in copies[4:]:
        copy.wait()
    out.wait()


def load(wq, wkt, wvt, wo, wg, wu, wdt):
    width, hidden = wg.shape
    *weights, joined_back = pl.pallas_call(
        load_kernel,
        out_shape=[
            pltpu.VMEM((3 * width, hidden), BF),
            pltpu.VMEM((3 * hidden + width, width), BF),
            pltpu.VMEM((width, JOINED), BF),
            pltpu.HBM((JOINED, width), BF),
        ],
        in_specs=[pl.BlockSpec(memory_space=pltpu.HBM)] * 7,
        out_specs=[vmem()] * 3 + [pl.BlockSpec(memory_space=pltpu.HBM)],
        scratch_shapes=[
            pltpu.VMEM(wq.shape, BF),
            pltpu.VMEM((JOINED, width), BF),
            pltpu.SemaphoreType.DMA((7,)),
            pltpu.SemaphoreType.DMA,
        ],
        compiler_params=pltpu.CompilerParams(vmem_limit_bytes=16 * MEGA),
        name="load_weights",
    )(*pinned((wq, wkt, wvt, wo, wg, wu, wdt)))
    return weights, joined_back


def turn_kernel(hidden, wide, tall, *rest):
    wot, vot, sem = rest[-3:]
    width = wot.shape[0]
    vg, vu, _ = wide_views(wide, width)
    _, vgt, vut, vo = tall_views(tall, hidden, width)
    vot[:, :width] = vo[...].T
    vot[:, width:] = jnp.zeros((width, HEAD), BF)
    out = pltpu.make_async_copy(vot, wot, sem)
    out.start()
    turn(vg, vgt)
    turn(vu, vut)
    out.wait()


def turned(wide, tall):
    hidden, width = wide.shape[1], tall.shape[1]
    return pl.pallas_call(
        functools.partial(turn_kernel, hidden),
        out_shape=vmem_like((wide, tall)) + [pltpu.HBM((width, CHUNKS * LANES), BF)],
        in_specs=[vmem()] * 2,
        out_specs=[vmem()] * 2 + [pl.BlockSpec(memory_space=pltpu.HBM)],
        scratch_shapes=[pltpu.VMEM((width, CHUNKS * LANES), BF), pltpu.SemaphoreType.DMA],
        input_output_aliases={0: 0, 1: 1},
        compiler_params=pltpu.CompilerParams(vmem_limit_bytes=16 * MEGA),
        name="turn_weights",
    )(*resident((wide, tall)))


def parts_kernel(normed, context, made, out, stage, sems):
    rows = normed.shape[0] * normed.shape[1]
    edge = QUERY + 2 * PAIR
    gets = [views(made, SLOPES, app)[0] for app in range(2)]
    attend, branch, first, second = (
        jnp.concatenate([get(name) for get in gets], axis=0) for name in ("attend", "branch", "first", "second")
    )

    def flat(ref):
        return ref[...].reshape(rows, ref.shape[2])

    half = 6 * LANES
    bounds = (0, half, JOINED, stage.shape[1])
    copies = [
        pltpu.make_async_copy(stage.at[:, pl.ds(low, high - low)], out.at[:, pl.ds(low, high - low)], sems.at[i])
        for i, (low, high) in enumerate(zip(bounds[:-1], bounds[1:]))
    ]
    left, right = flat(normed), attend
    stage[:, :half] = dot_first(left, right[:, :half]).astype(BF)
    copies[0].start()
    stage[:, half:JOINED] = dot_first(left, right[:, half:]).astype(BF)
    lanes = lax.broadcasted_iota(jnp.int32, (rows, HEAD), 1)
    gains = dot_first(first, (lanes == 0).astype(BF)) + dot_first(second, (lanes == 1).astype(BF))
    stage[:, edge:JOINED] = gains.astype(BF)
    copies[1].start()
    stage[:, JOINED : JOINED + QUERY] = dot_first(flat(context), branch).astype(BF)
    stage[:, JOINED + QUERY :] = jnp.zeros((QUERY, HEAD), BF)
    copies[2].start()
    for copy in copies:
        copy.wait()


def parts(normed, context, made):
    shape = (QUERY, JOINED + QUERY + HEAD)
    return pl.pallas_call(
        parts_kernel,
        out_shape=pltpu.HBM(shape, BF),
        in_specs=[vmem()] * 3,
        out_specs=pl.BlockSpec(memory_space=pltpu.HBM),
        scratch_shapes=[pltpu.VMEM(shape, BF), pltpu.SemaphoreType.DMA((3,))],
        compiler_params=pltpu.CompilerParams(vmem_limit_bytes=16 * MEGA),
        cost_estimate=pl.CostEstimate(flops=4 * shape[0] * shape[1] * normed.shape[0] * normed.shape[1], bytes_accessed=4 * shape[0] * shape[1], transcendentals=0),
        name="attention_parts",
    )(*resident((normed, context, made)))


def factors_kernel(second, wg, wu, gate_factor, up_factor, active):
    step = 256
    for i in range(second.shape[0] // step):
        band = slice(i * step, (i + 1) * step)
        block = second[band]
        gate = dot(block, wg[...])
        up = dot(block, wu[...])
        sigma = jax.nn.sigmoid(gate)
        linear = gate * sigma
        gate_factor[band] = (up * (sigma + linear * (1.0 - sigma))).astype(BF)
        up_factor[band] = linear.astype(BF)
        active[band] = (linear * up).astype(BF)


def factors(second, wg, wu):
    rows, width = second.shape
    hidden = wg.shape[1]
    block, piece = 512, 512
    wide = pl.BlockSpec((block, piece), lambda i, j: (j, i))
    weight = pl.BlockSpec((width, piece), lambda i, j: (0, i))
    return pl.pallas_call(
        factors_kernel,
        grid=(hidden // piece, rows // block),
        out_shape=[jax.ShapeDtypeStruct((rows, hidden), BF)] * 3,
        in_specs=[
            pl.BlockSpec((block, width), lambda i, j: (j, 0)),
            weight,
            weight,
        ],
        out_specs=[wide] * 3,
        compiler_params=pltpu.CompilerParams(vmem_limit_bytes=16 * MEGA),
        cost_estimate=pl.CostEstimate(flops=4 * rows * width * hidden, bytes_accessed=8 * rows * hidden, transcendentals=rows * hidden),
        name="feed_factors",
    )(second, wg, wu)


def feed_kernel(own, last, mixer, second, chosen, wdt, gate_factor, up_factor, active, *rest):
    earlier, (gate, up, down, squares) = rest[:-4], rest[-4:]
    blocks = mixer[...]
    mine = dot_last(chosen[...], blocks).astype(BF)
    second_own = dot_last(chosen[...], second[...]).astype(BF)
    piece = 512
    total = None
    for i in range(wdt.shape[1] // piece):
        cols = slice(i * piece, (i + 1) * piece)
        slope = dot(blocks, wdt[:, cols])
        gate_slope = (slope * gate_factor[:, cols].astype(F32)).astype(BF)
        up_slope = (slope * up_factor[:, cols].astype(F32)).astype(BF)
        parts = (dot(second_own, gate_slope), dot(second_own, up_slope), dot(mine, active[:, cols]))
        for k, (ref, part) in enumerate(zip((gate, up, down), parts)):
            part = part[:own]
            if earlier:
                part = part + earlier[k][:, cols]
            ref[:, cols] = part
            if last:
                square = jnp.sum(part * part, axis=0, keepdims=True)
                total = square if total is None else total + square
    squares[...] = total if last else jnp.zeros_like(squares)


def feed(own, last, mixer, second, chosen, wdt, made, earlier):
    hidden = wdt.shape[1]
    operands = (mixer, second, chosen, wdt, *made, *earlier)
    return pl.pallas_call(
        functools.partial(feed_kernel, own, last),
        out_shape=[jax.ShapeDtypeStruct((own, hidden), F32)] * 3 + [jax.ShapeDtypeStruct((1, 512), F32)],
        in_specs=[vmem()] * len(operands),
        out_specs=[vmem()] * 4,
        compiler_params=pltpu.CompilerParams(vmem_limit_bytes=16 * MEGA),
        cost_estimate=pl.CostEstimate(flops=2 * (mixer.shape[0] + 3 * own) * wdt.size, bytes_accessed=8 * mixer.shape[0] * hidden, transcendentals=0),
        name="feed_gradient",
    )(*resident(operands))


def after(value, *tokens):
    return lax.optimization_barrier((value,) + tokens)[0]


def gathered_at(block, axis, target):
    count = lax.axis_size(axis)
    pieces = [block if s == target else lax.ppermute(block, axis, [(s, target)]) for s in range(count)]
    return pieces


def spread_from(whole, axis, source):
    count = lax.axis_size(axis)
    width = whole.shape[1] // count
    columns = [whole[:, s * width : (s + 1) * width] for s in range(count)]
    mine = jnp.where(lax.axis_index(axis) == source, columns[source], jnp.zeros_like(columns[source]))
    for s in range(count):
        if s != source:
            mine = mine + lax.ppermute(columns[s], axis, [(source, s)])
    return mine


class LineGather:
    def __init__(self, block, axis):
        self.axis, self.count = axis, lax.axis_size(axis)
        self.line, self.step = self.count // 2, 0
        self.held = [block] + [None] * (self.line - 1)
        self.moving = (block, block)

    def advance(self, *tokens):
        ahead = [(i, i + 2) for i in range(self.count - 2)]
        self.step += 1
        below, above = self.moving
        if tokens:
            below, above, *_ = lax.optimization_barrier((below, above, *tokens))
        below = lax.ppermute(below, self.axis, ahead)
        above = lax.ppermute(above, self.axis, [(b, a) for a, b in ahead])
        self.moving = (below, above)
        for k, item in ((self.step, below), (self.line - self.step, above)):
            self.held[k] = item if self.held[k] is None else self.held[k] + item

    def finish(self):
        while self.step < self.line - 1:
            self.advance()
        mine = jnp.concatenate(self.held)
        other = lax.ppermute(mine, self.axis, [(i, i ^ 1) for i in range(self.count)])
        bands = [slice(start, start + BAND) for start in range(0, mine.shape[0], BAND)]
        return [half[band] for half in (mine, other) for band in bands]


def summed(value, axis):
    count, distance = lax.axis_size(axis), 1
    while distance < count:
        value = value + lax.ppermute(value, axis, [(i, i ^ distance) for i in range(count)])
        distance *= 2
    return value


def per_device(
    inputs, cotangent, first_gain, w_query, w_key, w_value, w_output, second_gain, w_gate, w_up, w_down
):
    sections = lax.axis_size("section")
    replicas = lax.axis_size("dp")
    section = lax.axis_index("section")
    micro, length, part = inputs.shape
    rows, width = micro * length, part * sections
    hidden = w_gate.shape[2]
    own = width // replicas
    w_query, w_key, w_value, w_output = w_query[0], w_key[0], w_value[0], w_output[0]
    w_gate, w_up, w_down = w_gate[0], w_up[0], w_down[0]
    gains = (first_gain, second_gain)
    tables = tuple(jnp.asarray(table) for table in rotary_tables(length, rows))
    place = section.astype(jnp.int32).reshape(1)
    w_query, place = lax.optimization_barrier((w_query, place))
    own_rows = -(-own // 16) * 16
    at = lax.broadcasted_iota(jnp.int32, (own_rows, width), 0)
    chosen = jnp.logical_and(
        lax.broadcasted_iota(jnp.int32, (own_rows, width), 1) == at + own * lax.axis_index("dp"), at < own
    ).astype(BF)

    x = gathered_at(inputs.reshape(rows, part), "section", 0)
    w_down = w_down.T
    weights, joined_back = load(w_query, w_key.T, w_value.T, w_output, w_gate, w_up, w_down)
    last_slope = gathered_at(cotangent.reshape(rows, part), "section", sections - 1)

    stash = lefts = ()
    for t in range(sections):
        final, leaving, weights, stash, lefts = forward_pass(
            t, place, x, gains, tables, weights, stash, lefts, length, hidden
        )
        if t < sections - 1:
            x = [lax.ppermute(leaving, "section", [(t, t + 1)])]
        if t == 0:
            *changed, output_back = turned(*weights[:2])
            weights = [*changed, weights[2]]
    normed, context, second = lefts
    streamed = (output_back, joined_back)
    weights = weights[:2]

    slope = last_slope
    made = mixers = behind = ()
    for t in reversed(range(sections)):
        entering, leaving, weights, stash, made, mixers = backward_pass(
            t, place, slope, gains, tables, stash, streamed, weights, made, mixers, length, hidden, behind
        )
        if t > 0:
            slope = [lax.ppermute(leaving, "section", [(t, t - 1)])]
        if t == sections - 1:
            outputs = spread_from(after(final, leaving).astype(BF), "section", sections - 1)
        if t > 0:
            if t == sections - 1:
                second_all = lax.all_gather(after(second.reshape(2 * rows, width), leaving), "dp", axis=0, tiled=True)
    slopes = made
    bands = [slice(start, start + BAND) for start in range(0, 2 * rows * replicas, BAND)]
    second_all = [second_all[band] for band in bands]
    mixer_all = lax.all_gather(mixers[0].reshape(2 * rows, width), "dp", axis=0, tiled=True)
    mixer_all = [mixer_all[band] for band in bands]
    delta_inputs = spread_from(leaving, "section", 0)
    terms = parts(normed, context, slopes[0])
    reduced = lax.psum_scatter(terms, "dp", scatter_dimension=0, tiled=True).astype(F32)
    made = [factors(second, w_gate, w_up) for second in second_all]
    feed_parts = ()
    for i, (mixer, second, item) in enumerate(zip(mixer_all, second_all, made)):
        last = i == len(made) - 1
        *feed_parts, squares = feed(own, last, mixer, second, chosen, w_down, item, feed_parts)
    gate, up, down = feed_parts
    total = jnp.sum(squares) + jnp.sum(reduced * reduced)
    total = summed(summed(total.reshape(1), "dp"), "section")
    edge = QUERY + 2 * PAIR
    return (
        outputs.astype(F32).reshape(micro, length, part),
        delta_inputs.astype(F32).reshape(micro, length, part),
        reduced[:, edge][None],
        reduced[:, :QUERY][None],
        reduced[:, QUERY : QUERY + PAIR][None],
        reduced[:, QUERY + PAIR : edge][None],
        reduced[:, JOINED : JOINED + QUERY][None],
        reduced[:, edge + 1][None],
        gate[None],
        up[None],
        down.T[None],
        jnp.sqrt(total).reshape(()),
    )


def solution(mesh):
    stacked = P("section", None, None)
    rows = P("section", "dp", None)
    return jax.shard_map(
        per_device,
        mesh=mesh,
        in_specs=(P("dp", None, "section"),) * 2
        + (P("section", None),)
        + (stacked,) * 4
        + (P("section", None),)
        + (stacked,) * 3,
        out_specs=(P("dp", None, "section"),) * 2
        + (P("section", "dp"),)
        + (rows,) * 4
        + (P("section", "dp"),)
        + (rows,) * 2
        + (P("section", None, "dp"), P()),
        check_vma=False,
    )
```

time: 2200 us -> 360 us (0.16)
  waiting for transfers between devices: 615 us -> 98.1 us
  local copies, waits for them, and re-layouts: 508 us -> 81.9 us
  matrix products: 382 us -> 0 us
  other arithmetic: 367 us -> 5.19 us
  starting transfers between devices: 226 us -> 35.7 us
  Pallas kernels: 0 us -> 114 us
  blocking collectives: 65.8 us -> 0 us
    dot_general x184 -> x0, matrix products: 382 us -> none  [the longest x16 117 us: outer_sum(): lax.dot_general(left, right, (((0,), (0,)), ((), ())), preferred_element_...]
    ppermute x14 -> x23, waiting for transfers between devices: 459 us -> 98.1 us  [the longest x3 90.5 us: per_device(): slope = [lax.ppermute(leaving, 'section', [(t, t - 1)])]]
    all_to_all x8 -> x0, waiting for transfers between devices: 156 us -> none  [the longest x1 132 us: per_device(): lax.all_to_all(members[4].astype(jnp.bfloat16), 'dp', split_axis=1, conca...]
    ppermute x14 -> x23, starting transfers between devices: 191 us -> 35.6 us  [the longest x5 13 us: summed(): lax.ppermute(value, axis, [(i, i ^ distance) for i in range(count)])]
    unnamed x4 -> x1, other arithmetic: 123 us -> 0.01 us
    convert_element_type x50 -> x0, local copies, waits for them, and re-layouts: 119 us -> none  [the longest x1 48.8 us: per_device(): members[4].astype(jnp.bfloat16)]
    convert_element_type x94 -> x3, other arithmetic: 120 us -> 2.14 us  [the longest x1 1.24 us: per_device(): lax.psum_scatter(terms, 'dp', scatter_dimension=0, tiled=True).astype(F32)]
    pallas_call x0 -> x15, Pallas kernels: none -> 114 us  [the longest x2 30.8 us: factors(): pl.pallas_call(factors_kernel, grid=(hidden // piece, rows // block), out...]
  transfers between devices with their start and end apart: 22 -> 26, of which waited for: 18 -> 8; matrix products, arithmetic and copies ran while one was open for 17% -> 2% of each run, Pallas kernels for 0% -> 26%
where the time goes in v1:
time: 360 us; the launch traced here: 356 us
  Pallas kernels  114 us (32%)
  waiting for transfers between devices  98.1 us (27%)
  local copies, waits for them, and re-layouts  81.9 us (23%)
  starting transfers between devices  35.7 us (10%)
  between operations  20.6 us (6%)
  other arithmetic  5.19 us (1%)
    ppermute x3, waiting for transfers between devices, per_device(): slope = [lax.ppermute(leaving, 'section', [(t, t - 1)])]  90.5 us
    unnamed x94, local copies, waits for them, and re-layouts  74.2 us
    pallas_call x2, Pallas kernels, factors(): pl.pallas_call(factors_kernel, grid=(hidden // piece, rows // block), out...  30.8 us
    pallas_call x4, Pallas kernels, backward_pass(): pl.pallas_call(functools.partial(backward_kernel, tick, rows, length, hid...  27.7 us
    pallas_call x2, Pallas kernels, feed(): pl.pallas_call(functools.partial(feed_kernel, own, last), out_shape=[jax....  22.3 us
    pallas_call x4, Pallas kernels, forward_pass(): pl.pallas_call(functools.partial(forward_kernel, tick, rows, length, hidd...  18.1 us
    ppermute x5, starting transfers between devices, summed(): lax.ppermute(value, axis, [(i, i ^ distance) for i in range(count)])  13 us
    ppermute x6, starting transfers between devices, spread_from(): mine = mine + lax.ppermute(columns[s], axis, [(source, s)])  10.7 us
  transfers between devices with their start and end apart: 26, of which 8 were waited for; matrix products, arithmetic and copies ran while one was open for 2% of the time, Pallas kernels for 26%

profile of v1, /device:TPU:0, one launch (start us, length us, event | category | flops | bytes accessed | tf_op | source)
XLA Modules:
  0.0 355.7 jit_solution(5706563388415466764)
XLA Ops:
  11.2 8.1 %load_weights.1 = (bf16[2880,2560]{1,0:T(8,128)(2,1)S(1)}, bf16[8640,960]{1,0:T(8,128)(2,1)S(1)}, bf16[960,1664]{1,0:T(8,128)(2,1)S(1)}, bf16[1664,960]{1,0:T(8,128)(2,1)}) custom-call(bf16[960,960]{1,0:T(8,128)(2,1)} %bitcast.61, bf16[320,960]{1,0:T(8,128)(2,1)} %bitcast.63, bf16[320,960]{1,0:T(8,128)(2,1)} %bitcast.64, bf16[960,960]{1,0:T(8,128)(2,1)} %bitcast.62, ...), custom_call_target="tpu_custom_call" | custom-call | tf_op jit(solution)/shard_map/load_weights/pallas_call | solution.py:466
  19.4 12.5 %forward_pass.4 = (f32[128,960]{1,0:T(8,128)}, bf16[128,960]{1,0:T(8,128)(2,1)}, bf16[2880,2560]{1,0:T(8,128)(2,1)S(1)}, bf16[8640,960]{1,0:T(8,128)(2,1)S(1)}, ...) custom-call(s32[1]{0:T(128)} %bitcast.1.section, ...), custom_call_target="tpu_custom_call", output_to_operand_aliasing={{2}: (9, {}), {3}: (10, {}), {4}: (11, {})} | custom-call | tf_op jit(solution)/shard_map/forward_pass/pallas_call | solution.py:248
  31.8 1.5 collective-permute-start.3
  33.4 3.5 turn_weights.1
  36.8 3.1 collective-permute-done.3.rest_0_
  41.5 1.4 forward_pass.6
  46.3 3.4 forward_pass.7
  49.7 7.1 %backward_pass.4 = (f32[128,960]{1,0:T(8,128)}, bf16[128,960]{1,0:T(8,128)(2,1)}, bf16[2880,2560]{1,0:T(8,128)(2,1)S(1)}, bf16[8640,960]{1,0:T(8,128)(2,1)S(1)},...) custom-call(s32[1]{0:T(128)} %bitcast.1.section, ...), custom_call_target="tpu_custom_call", output_to_operand_aliasing={{2}: (11, {}), {3}: (12, {}), {4}: (13, {}), {5}: (14, {})} | custom-call | tf_op jit(solution)/shard_map/backward_pass/pallas_call | solution.py:397
  56.8 6.1 %copy-done = bf16[8640,960]{1,0:T(8,128)(2,1)} copy-done((bf16[8640,960]{1,0:T(8,128)(2,1)}, bf16[8640,960]{1,0:T(8,128)(2,1)S(1)}, u32[]{:S(2)}) %copy-start) | copy-done | bytes 16588824
  62.9 5.1 %copy-done.2 = bf16[2880,2560]{1,0:T(8,128)(2,1)} copy-done((bf16[2880,2560]{1,0:T(8,128)(2,1)}, bf16[2880,2560]{1,0:T(8,128)(2,1)S(1)}, u32[]{:S(2)}) %copy-start.2) | copy-done | bytes 14745624
  68.0 2.4 copy-done.4
  71.7 1.4 copy-done.8
  73.9 6.0 %copy-done.1 = bf16[8640,960]{1,0:T(8,128)(2,1)S(1)} copy-done((bf16[8640,960]{1,0:T(8,128)(2,1)S(1)}, bf16[8640,960]{1,0:T(8,128)(2,1)}, u32[]{:S(2)}) %copy-start.1) | copy-done | bytes 16588824
  79.9 5.2 %copy-done.3 = bf16[2880,2560]{1,0:T(8,128)(2,1)S(1)} copy-done((bf16[2880,2560]{1,0:T(8,128)(2,1)S(1)}, bf16[2880,2560]{1,0:T(8,128)(2,1)}, u32[]{:S(2)}) %copy-start.3) | copy-done | bytes 14745624
  85.1 2.6 copy-done.5
  87.7 1.6 copy-done.7
  89.3 1.7 copy-done.9
  93.0 6.3 %backward_pass.6 = (f32[128,960]{1,0:T(8,128)}, bf16[128,960]{1,0:T(8,128)(2,1)}, bf16[2880,2560]{1,0:T(8,128)(2,1)S(1)}, bf16[8640,960]{1,0:T(8,128)(2,1)S(1)},...) custom-call(s32[1]{0:T(128)} %bitcast.1.section, ...), custom_call_target="tpu_custom_call", output_to_operand_aliasing={{2}: (8, {}), {3}: (9, {}), {4}: (10, {}), {5}: (11, {}), {... | custom-call | tf_op jit(solution)/shard_map/backward_pass/pallas_call | solution.py:397
  100.5 90.5 %collective-permute-done.14.rest_0_ = bf16[128,960]{1,0:T(8,128)(2,1)S(1)} collective-permute-done((bf16[128,960]{1,0:T(8,128)(2,1)}, bf16[128,960]{1,0:T(8,128)(2,1)S(1)}, u32[]{:S(2)}, u32[]{:S(2)}) %collective-permute-start.14) | collective-permute-done | bytes 245792 | tf_op jit(solution)/shard_map/ppermute | solution.py:741
  191.0 13.1 %backward_pass.7 = (f32[128,960]{1,0:T(8,128)}, bf16[128,960]{1,0:T(8,128)(2,1)}, bf16[2880,2560]{1,0:T(8,128)(2,1)S(1)}, bf16[8640,960]{1,0:T(8,128)(2,1)S(1)},...) custom-call(s32[1]{0:T(128)} %bitcast.1.section, ...), custom_call_target="tpu_custom_call", output_to_operand_aliasing={{2}: (8, {}), {3}: (9, {}), {4}: (10, {}), {5}: (11, {}), {... | custom-call | tf_op jit(solution)/shard_map/backward_pass/pallas_call | solution.py:397
  204.1 1.4 copy-done.10
  205.6 1.7 copy-done.11
  207.2 3.7 %attention_parts.1 = bf16[960,2688]{1,0:T(8,128)(2,1)} custom-call(bf16[2,128,960]{2,1,0:T(8,128)(2,1)S(1)} %copy-done.20, bf16[2,128,960]{2,1,0:T(8,128)(2,1)S(1)} %copy-done.21, bf16[2,128,4736]{2,1,0:T(8,128)(2,1)S(1)} %copy-done.11), custom_call_target="tpu_custom_call" | custom-call | flops 2642411520 | bytes 10321920 | tf_op jit(solution)/shard_map/attention_parts/pallas_call | solution.py:550
  215.0 5.4 %collective-permute-start.17 = (bf16[128,240]{1,0:T(8,128)(2,1)S(1)}, bf16[128,240]{1,0:T(8,128)(2,1)S(1)}, u32[]{:S(2)}, u32[]{:S(2)}) collective-permute-start(bf16[128,240]{1,0:T(8,128)(2,1)S(1)} %get-tuple-element.225), channel_id=1, source_target_pairs={{0,24},{1,25},{2,26},{3,27},{4,28},{5,29},{6,30},{7,31}} | collective-permute-start | bytes 184328 | tf_op jit(solution)/shard_map/ppermute | solution.py:653
  225.6 2.7 fusion.5
  228.4 3.2 copy-done.18
  231.5 2.4 copy-done.19
  234.0 15.3 %feed_factors.2 = (bf16[1024,2560]{1,0:T(8,128)(2,1)S(1)}, bf16[1024,2560]{1,0:T(8,128)(2,1)S(1)}, bf16[1024,2560]{1,0:T(8,128)(2,1)S(1)}) custom-call(bf16[1024,960]{1,0:T(8,128)(2,1)S(1)} %get-tuple-element.217.second, bf16[960,2560]{1,0:T(8,128)(2,1)S(1)} %bitcast.46, bf16[960,2560]{1,0:T(8,128)(2,1)S(1)} %bitcast.49), custom_call_target="tpu_custom_call" | custom-call | flops 10066329600 | bytes 20971520 | tf_op jit(solution)/shard_map/feed_factors/pallas_call | solution.py:582
  249.3 2.3 copy-done.13
  251.6 2.4 copy-done.14
  254.0 2.3 copy-done.16
  256.3 15.5 %feed_factors.3 = (bf16[1024,2560]{1,0:T(8,128)(2,1)S(1)}, bf16[1024,2560]{1,0:T(8,128)(2,1)S(1)}, bf16[1024,2560]{1,0:T(8,128)(2,1)S(1)}) custom-call(bf16[1024,960]{1,0:T(8,128)(2,1)S(1)} %get-tuple-element.216.second, bf16[960,2560]{1,0:T(8,128)(2,1)S(1)} %bitcast.47, bf16[960,2560]{1,0:T(8,128)(2,1)S(1)} %bitcast.50), custom_call_target="tpu_custom_call" | custom-call | flops 10066329600 | bytes 20971520 | tf_op jit(solution)/shard_map/feed_factors/pallas_call | solution.py:582
  271.8 2.3 copy-done.35
  274.1 2.4 copy-done.37
  276.5 2.3 copy-done.39
  278.8 2.9 fusion.6
  281.8 2.4 copy-done.12
  284.2 1.6 copy-done.25
  285.8 2.6 copy-done.36
  288.3 2.5 copy-done.38
  290.9 2.5 copy-done.40
  293.4 10.2 %feed_gradient.2 = (f32[120,2560]{1,0:T(8,128)S(1)}, f32[120,2560]{1,0:T(8,128)S(1)}, f32[120,2560]{1,0:T(8,128)S(1)}, f32[1,512]{1,0:T(1,128)}) custom-call(bf16[1024,960]{1,0:T(8,128)(2,1)S(1)} %get-tuple-element.218.mixer, bf16[1024,960]{1,0:T(8,128)(2,1)S(1)} %copy-done.25, bf16[128,960]{1,0:T(8,128)(2,1)S(1)} %copy-done.30, ...), custom_call_target="tpu_custom_call" | custom-call | flops 6802636800 | bytes 20971520 | tf_op jit(solution)/shard_map/feed_gradient/pallas_call | solution.py:625
  306.9 1.3 copy-done.29
  308.3 12.1 %feed_gradient.3 = (f32[120,2560]{1,0:T(8,128)}, f32[120,2560]{1,0:T(8,128)}, f32[120,2560]{1,0:T(8,128)}, f32[1,512]{1,0:T(1,128)S(1)}) custom-call(bf16[1024,960]{1,0:T(8,128)(2,1)S(1)} %get-tuple-element.219.mixer, bf16[1024,960]{1,0:T(8,128)(2,1)S(1)} %get-tuple-element.217.second, bf16[128,960]{1,0:T(8,128)(2,1)S(1)} %copy-done.30, ...), custom_call_target="tpu_custom_call" | custom-call | flops 6802636800 | bytes 20971520 | tf_op jit(solution)/shard_map/feed_gradient/pallas_call | solution.py:625
  329.8 2.6 collective-permute-start.19
  334.1 3.5 collective-permute-start.20
  339.2 3.5 collective-permute-start.21
  343.5 2.5 collective-permute-start.22
  (135 shorter events, 37.3 us)
Async XLA Ops:
  7.2 218.4 %all-gather.5.cloned.1.call-start = ((), (), s32[]{:S(2)}) async-start(), calls=%async_computation.2 | async-start | bytes 4718592 | tf_op jit(solution)/shard_map/all_gather | solution.py:746
  7.2 12.1 %collective-permute-start = (bf16[128,240]{1,0:T(8,128)(2,1)}, bf16[128,240]{1,0:T(8,128)(2,1)S(1)}, u32[]{:S(2)}, u32[]{:S(2)}) collective-permute-start(bf16[128,240]{1,0:T(8,128)(2,1)} %bitcast.51), channel_id=1, source_target_pairs={{8,0},{9,1},{10,2},{11,3},{12,4},{13,5},{14,6},{15,7}} | collective-permute-start | bytes 184328 | tf_op jit(solution)/shard_map/ppermute | solution.py:642
  8.5 10.8 %collective-permute-start.1 = (bf16[128,240]{1,0:T(8,128)(2,1)}, bf16[128,240]{1,0:T(8,128)(2,1)S(1)}, u32[]{:S(2)}, u32[]{:S(2)}) collective-permute-start(bf16[128,240]{1,0:T(8,128)(2,1)} %bitcast.52), channel_id=1, source_target_pairs={{16,0},{17,1},{18,2},{19,3},{20,4},{21,5},{22,6},{23,7}} | collective-permute-start | bytes 184328 | tf_op jit(solution)/shard_map/ppermute | solution.py:642
  9.8 9.5 %collective-permute-start.2 = (bf16[128,240]{1,0:T(8,128)(2,1)}, bf16[128,240]{1,0:T(8,128)(2,1)S(1)}, u32[]{:S(2)}, u32[]{:S(2)}) collective-permute-start(bf16[128,240]{1,0:T(8,128)(2,1)} %bitcast.53), channel_id=1, source_target_pairs={{24,0},{25,1},{26,2},{27,3},{28,4},{29,5},{30,6},{31,7}} | collective-permute-start | bytes 184328 | tf_op jit(solution)/shard_map/ppermute | solution.py:642
  11.1 8.2 %copy-start.22 = (f32[128,128]{1,0:T(8,128)S(1)}, f32[128,128]{1,0:T(8,128)}, u32[]{:S(2)}) copy-start(f32[128,128]{1,0:T(8,128)} %constant.23.clone.cosine) | copy-start | bytes 196612
  11.1 8.2 %copy-start.23 = (f32[128,128]{1,0:T(8,128)S(1)}, f32[128,128]{1,0:T(8,128)}, u32[]{:S(2)}) copy-start(f32[128,128]{1,0:T(8,128)} %constant.24.clone.sine) | copy-start | bytes 196612
  11.2 8.2 %copy-start.31 = (f32[1,960]{1,0:T(1,128)S(1)}, f32[1,960]{1,0:T(1,128)}, u32[]{:S(2)}) copy-start(f32[1,960]{1,0:T(1,128)} %gain_one.15) | copy-start | bytes 11524
  11.2 8.2 %copy-start.32 = (f32[1,960]{1,0:T(1,128)S(1)}, f32[1,960]{1,0:T(1,128)}, u32[]{:S(2)}) copy-start(f32[1,960]{1,0:T(1,128)} %gain_two.15) | copy-start | bytes 11524
  11.2 8.2 %copy-start.33 = (bf16[4,32,240]{2,1,0:T(8,128)(2,1)S(1)}, bf16[4,32,240]{2,1,0:T(8,128)(2,1)}, u32[]{:S(2)}) copy-start(bf16[4,32,240]{2,1,0:T(8,128)(2,1)} %param.13) | copy-start | bytes 184324
  31.8 8.1 %collective-permute-start.3 = (bf16[128,960]{1,0:T(8,128)(2,1)}, bf16[128,960]{1,0:T(8,128)(2,1)S(1)}, u32[]{:S(2)}, u32[]{:S(2)}) collective-permute-start(bf16[128,960]{1,0:T(8,128)(2,1)} %get-tuple-element.100), channel_id=1, source_target_pairs={{0,8},{1,9},{2,10},{3,11},{4,12},{5,13},{6,14},{7,15}} | collective-permute-start | bytes 737288 | tf_op jit(solution)/shard_map/ppermute | solution.py:726
  40.8 0.7 collective-permute-start.4
  42.9 3.3 collective-permute-start.5
  43.6 6.0 %collective-permute-start.6 = (bf16[128,240]{1,0:T(8,128)(2,1)S(1)}, bf16[128,240]{1,0:T(8,128)(2,1)S(1)}, u32[]{:S(2)}, u32[]{:S(2)}) collective-permute-start(bf16[128,240]{1,0:T(8,128)(2,1)S(1)} %bitcast.55), channel_id=1, source_target_pairs={{0,24},{1,25},{2,26},{3,27},{4,28},{5,29},{6,30},{7,31}} | collective-permute-start | bytes 184328 | tf_op jit(solution)/shard_map/ppermute | solution.py:642
  44.9 4.7 %collective-permute-start.7 = (bf16[128,240]{1,0:T(8,128)(2,1)S(1)}, bf16[128,240]{1,0:T(8,128)(2,1)S(1)}, u32[]{:S(2)}, u32[]{:S(2)}) collective-permute-start(bf16[128,240]{1,0:T(8,128)(2,1)S(1)} %bitcast.56), channel_id=1, source_target_pairs={{8,24},{9,25},{10,26},{11,27},{12,28},{13,29},{14,30},{15,31}} | collective-permute-start | bytes 184328 | tf_op jit(solution)/shard_map/ppermute | solution.py:642
  45.6 4.1 %collective-permute-start.8 = (bf16[128,240]{1,0:T(8,128)(2,1)S(1)}, bf16[128,240]{1,0:T(8,128)(2,1)S(1)}, u32[]{:S(2)}, u32[]{:S(2)}) collective-permute-start(bf16[128,240]{1,0:T(8,128)(2,1)S(1)} %bitcast.57), channel_id=1, source_target_pairs={{16,24},{17,25},{18,26},{19,27},{20,28},{21,29},{22,30},{23,31}} | collective-permute-start | bytes 184328 | tf_op jit(solution)/shard_map/ppermute | solution.py:642
  56.8 6.1 %copy-start = (bf16[8640,960]{1,0:T(8,128)(2,1)}, bf16[8640,960]{1,0:T(8,128)(2,1)S(1)}, u32[]{:S(2)}) copy-start(bf16[8640,960]{1,0:T(8,128)(2,1)S(1)} %get-tuple-element.139.rest_4_) | copy-start | bytes 49766404
  62.9 5.1 %copy-start.2 = (bf16[2880,2560]{1,0:T(8,128)(2,1)}, bf16[2880,2560]{1,0:T(8,128)(2,1)S(1)}, u32[]{:S(2)}) copy-start(bf16[2880,2560]{1,0:T(8,128)(2,1)S(1)} %get-tuple-element.138.rest_3_) | copy-start | bytes 44236804
  73.2 205.7 %all-gather.3.cloned.1.call-start = ((), (), s32[]{:S(2)}) async-start(), calls=%async_computation.1 | async-start | bytes 4718592 | tf_op jit(solution)/shard_map/all_gather | solution.py:750
  73.2 0.7 collective-permute-start.12
  73.9 6.0 %copy-start.1 = (bf16[8640,960]{1,0:T(8,128)(2,1)S(1)}, bf16[8640,960]{1,0:T(8,128)(2,1)}, u32[]{:S(2)}) copy-start(bf16[8640,960]{1,0:T(8,128)(2,1)} %copy-done) | copy-start | bytes 49766404
  79.9 5.2 %copy-start.3 = (bf16[2880,2560]{1,0:T(8,128)(2,1)S(1)}, bf16[2880,2560]{1,0:T(8,128)(2,1)}, u32[]{:S(2)}) copy-start(bf16[2880,2560]{1,0:T(8,128)(2,1)} %copy-done.2) | copy-start | bytes 44236804
  85.1 2.6 copy-start.5
  92.3 0.7 collective-permute-start.13
  99.2 91.8 %collective-permute-start.14 = (bf16[128,960]{1,0:T(8,128)(2,1)}, bf16[128,960]{1,0:T(8,128)(2,1)S(1)}, u32[]{:S(2)}, u32[]{:S(2)}) collective-permute-start(bf16[128,960]{1,0:T(8,128)(2,1)} %get-tuple-element.151), channel_id=1, source_target_pairs={{8,0},{9,1},{10,2},{11,3},{12,4},{13,5},{14,6},{15,7}} | collective-permute-start | bytes 737288 | tf_op jit(solution)/shard_map/ppermute | solution.py:741
  191.0 14.6 %copy-start.20 = (bf16[2,128,960]{2,1,0:T(8,128)(2,1)S(1)}, bf16[2,128,960]{2,1,0:T(8,128)(2,1)}, u32[]{:S(2)}) copy-start(bf16[2,128,960]{2,1,0:T(8,128)(2,1)} %get-tuple-element.159.normed) | copy-start | bytes 1474564
  191.0 14.6 %copy-start.21 = (bf16[2,128,960]{2,1,0:T(8,128)(2,1)S(1)}, bf16[2,128,960]{2,1,0:T(8,128)(2,1)}, u32[]{:S(2)}) copy-start(bf16[2,128,960]{2,1,0:T(8,128)(2,1)} %get-tuple-element.160.context) | copy-start | bytes 1474564
  205.5 115.5 %reduce-scatter.4.cloned.1.call-start = ((), (), s32[]{:S(2)}) async-start(), calls=%async_computation.3 | async-start | bytes 5806080
  211.0 3.9 %copy-start.43 = (bf16[128,960]{1,0:T(8,128)(2,1)S(1)}, bf16[128,960]{1,0:T(8,128)(2,1)}, u32[]{:S(2)}) copy-start(bf16[128,960]{1,0:T(8,128)(2,1)} %get-tuple-element.158) | copy-start | bytes 737284
  212.2 9.5 %collective-permute-start.11 = (bf16[128,240]{1,0:T(8,128)(2,1)S(1)}, bf16[128,240]{1,0:T(8,128)(2,1)S(1)}, u32[]{:S(2)}, u32[]{:S(2)}) collective-permute-start(bf16[128,240]{1,0:T(8,128)(2,1)S(1)} %get-tuple-element.228), channel_id=1, source_target_pairs={{24,16},{25,17},{26,18},{27,19},{28,20},{29,21},{30,22},{31,23}} | collective-permute-start | bytes 184328 | tf_op jit(solution)/shard_map/ppermute | solution.py:653
  212.9 10.2 %collective-permute-start.10 = (bf16[128,240]{1,0:T(8,128)(2,1)S(1)}, bf16[128,240]{1,0:T(8,128)(2,1)S(1)}, u32[]{:S(2)}, u32[]{:S(2)}) collective-permute-start(bf16[128,240]{1,0:T(8,128)(2,1)S(1)} %get-tuple-element.229), channel_id=1, source_target_pairs={{24,8},{25,9},{26,10},{27,11},{28,12},{29,13},{30,14},{31,15}} | collective-permute-start | bytes 184328 | tf_op jit(solution)/shard_map/ppermute | solution.py:653
  213.5 9.5 %collective-permute-start.9 = (bf16[128,240]{1,0:T(8,128)(2,1)S(1)}, bf16[128,240]{1,0:T(8,128)(2,1)S(1)}, u32[]{:S(2)}, u32[]{:S(2)}) collective-permute-start(bf16[128,240]{1,0:T(8,128)(2,1)S(1)} %get-tuple-element.227), channel_id=1, source_target_pairs={{24,0},{25,1},{26,2},{27,3},{28,4},{29,5},{30,6},{31,7}} | collective-permute-start | bytes 184328 | tf_op jit(solution)/shard_map/ppermute | solution.py:653
  215.0 8.9 %collective-permute-start.17 = (bf16[128,240]{1,0:T(8,128)(2,1)S(1)}, bf16[128,240]{1,0:T(8,128)(2,1)S(1)}, u32[]{:S(2)}, u32[]{:S(2)}) collective-permute-start(bf16[128,240]{1,0:T(8,128)(2,1)S(1)} %get-tuple-element.225), channel_id=1, source_target_pairs={{0,24},{1,25},{2,26},{3,27},{4,28},{5,29},{6,30},{7,31}} | collective-permute-start | bytes 184328 | tf_op jit(solution)/shard_map/ppermute | solution.py:653
  220.4 3.4 collective-permute-start.16
  221.7 3.2 collective-permute-start.15
  228.4 27.9 %copy-start.24 = (bf16[1024,960]{1,0:T(8,128)(2,1)}, bf16[1024,960]{1,0:T(8,128)(2,1)S(1)}, u32[]{:S(2)}) copy-start(bf16[1024,960]{1,0:T(8,128)(2,1)S(1)} %get-tuple-element.216.second) | copy-start | bytes 5898244
  228.4 3.2 copy-start.18
  278.8 2.9 copy-start.30
  278.8 26.8 %slice-start = ((s8[5242880]{0:T(1024)(128)(4,1)}), s8[4194304]{0:T(1024)(128)(4,1)S(1)}, s32[]{:S(2)}) async-start(s8[5242880]{0:T(1024)(128)(4,1)} %bitcast.43), calls=%async_computation.4 | async-start | bytes 8388608
  285.8 2.6 copy-start.36
  293.4 12.2 %slice-start.1 = ((s8[5242880]{0:T(1024)(128)(4,1)}), s8[1048576]{0:T(1024)(128)(4,1)S(1)}, s32[]{:S(2)}) async-start(s8[5242880]{0:T(1024)(128)(4,1)} %bitcast.43), calls=%async_computation.5 | async-start | bytes 2097152
  293.4 12.2 %copy-start.15 = (bf16[1024,2560]{1,0:T(8,128)(2,1)S(1)}, bf16[1024,2560]{1,0:T(8,128)(2,1)}, u32[]{:S(2)}) copy-start(bf16[1024,2560]{1,0:T(8,128)(2,1)} %copy-done.14) | copy-start | bytes 15728644
  293.4 12.2 %copy-start.17 = (bf16[1024,2560]{1,0:T(8,128)(2,1)S(1)}, bf16[1024,2560]{1,0:T(8,128)(2,1)}, u32[]{:S(2)}) copy-start(bf16[1024,2560]{1,0:T(8,128)(2,1)} %copy-done.16) | copy-start | bytes 15728644
  321.0 4.7 %copy-start.41 = (bf16[120,2688]{1,0:T(8,128)(2,1)S(1)}, bf16[120,2688]{1,0:T(8,128)(2,1)}, u32[]{:S(2)}) copy-start(bf16[120,2688]{1,0:T(8,128)(2,1)} %reduce-scatter.4.cloned.1.call-done) | copy-start | bytes 1935364
  328.0 1.2 collective-permute-start.18
  329.8 3.6 %collective-permute-start.19 = (f32[1]{0:T(128)}, f32[1]{0:T(128)}, u32[]{:S(2)}, u32[]{:S(2)}) collective-permute-start(f32[1]{0:T(128)} %add.54), channel_id=1, source_target_pairs={{0,2},{1,3},{2,0},{3,1},{4,6},{5,7},{6,4},{7,5},{8,10},{9,11},{10,... | collective-permute-start | bytes 20 | tf_op jit(solution)/shard_map/ppermute | solution.py:688
  334.1 4.5 %collective-permute-start.20 = (f32[1]{0:T(128)}, f32[1]{0:T(128)}, u32[]{:S(2)}, u32[]{:S(2)}) collective-permute-start(f32[1]{0:T(128)} %add.55), channel_id=1, source_target_pairs={{0,4},{1,5},{2,6},{3,7},{4,0},{5,1},{6,2},{7,3},{8,12},{9,13},{10,... | collective-permute-start | bytes 20 | tf_op jit(solution)/shard_map/ppermute | solution.py:688
  339.2 3.7 %collective-permute-start.21 = (f32[1]{0:T(128)}, f32[1]{0:T(128)}, u32[]{:S(2)}, u32[]{:S(2)}) collective-permute-start(f32[1]{0:T(128)} %add.56), channel_id=1, source_target_pairs={{0,8},{8,0},{16,24},{24,16},{1,9},{9,1},{17,25},{25,17},{2,10},{10... | collective-permute-start | bytes 20 | tf_op jit(solution)/shard_map/ppermute | solution.py:688
  343.5 3.6 %collective-permute-start.22 = (f32[1]{0:T(128)}, f32[1]{0:T(128)}, u32[]{:S(2)}, u32[]{:S(2)}) collective-permute-start(f32[1]{0:T(128)} %add.57), channel_id=1, source_target_pairs={{0,16},{8,24},{16,0},{24,8},{1,17},{9,25},{17,1},{25,9},{2,18},{10... | collective-permute-start | bytes 20 | tf_op jit(solution)/shard_map/ppermute | solution.py:688
  (24 other events, 44.9 us)
Sparse Core Ops, SparseCore 0:
  73.3 99.8 all-gather.4
  205.6 46.0 all-gather.2
  254.0 57.9 reduce-scatter.3

commit v2 on v1

--- a/solution.py
+++ b/solution.py
@@ -89,12 +89,9 @@
 LEFTS = ("normed", "context", "second")
 
 
-def wide_views(wide, width):
-    return [wide.at[pl.ds(i * width, width)] for i in range(3)]
-
-
-def tall_views(tall, hidden, width):
-    return [tall.at[pl.ds(i * hidden, size)] for i, size in enumerate((hidden, hidden, hidden, width))]
+def halves(ref, *sizes):
+    starts = [sum(sizes[:i]) for i in range(len(sizes))]
+    return [ref.at[pl.ds(start, size)] for start, size in zip(starts, sizes)]
 
 
 def stash_widths(hidden):
@@ -134,11 +131,11 @@
 
 def forward_kernel(tick, rows, length, hidden, old, count, section, gain_one, gain_two, cosine, sine, *rest):
     x, rest = rest[:count], rest[count:]
-    (wide, tall, vqkv), (result, leaving), rest = rest[:3], rest[3 + old : 5 + old], rest[8 + old :]
-    stash, sums, *left_out, left, left_sems = rest
+    (wide, tall, vqkv), (result, leaving) = rest[:3], rest[old : old + 2]
+    stash, sums, *left_out, left, left_sems = rest[-7:]
     width = result.shape[1]
-    vg, vu, _ = wide_views(wide, width)
-    vd, _, _, vo = tall_views(tall, hidden, width)
+    vg, vu, _ = halves(wide, width, width, width)
+    vd, _, _, vo = halves(tall, hidden, hidden, hidden, width)
     piece = hidden // PIECES
 
     @pl.when(section[0] == tick)
@@ -246,7 +243,7 @@
     held = [*weights, *stash]
     count = len(x)
     outs = pl.pallas_call(
-        functools.partial(forward_kernel, tick, rows, length, hidden, len(stash) + len(lefts), count),
+        functools.partial(forward_kernel, tick, rows, length, hidden, len(held) + len(lefts), count),
         out_shape=[
             jax.ShapeDtypeStruct((rows, width), F32),
             jax.ShapeDtypeStruct((rows, width), BF),
@@ -257,7 +254,7 @@
         in_specs=[pl.BlockSpec(memory_space=pltpu.SMEM)]
         + [vmem()] * (4 + count + len(held))
         + [pl.BlockSpec(memory_space=pltpu.HBM)] * len(lefts),
-        out_specs=[vmem()] * 7 + [pl.BlockSpec(memory_space=pltpu.HBM)] * len(LEFTS),
+        out_specs=[vmem()] * (4 + len(weights)) + [pl.BlockSpec(memory_space=pltpu.HBM)] * len(LEFTS),
         scratch_shapes=[
             pltpu.VMEM((len(LEFTS), 2, rows, width), BF),
             pltpu.SemaphoreType.DMA((len(LEFTS), 2)),
@@ -266,20 +263,28 @@
         compiler_params=pltpu.CompilerParams(vmem_limit_bytes=16 * MEGA),
         name="forward_pass",
     )(section, *resident((*gains, *tables, *x, *held)), *pinned(lefts))
-    return outs[0], outs[1], outs[2:5], outs[5:7], outs[7:]
+    first = 2 + len(weights)
+    return outs[0], outs[1], outs[2:first], outs[first : first + 2], outs[first + 2 :]
 
 
 SLOPES = {"branch": QUERY, "attend": JOINED, "first": QUERY, "second": QUERY}
 SLOPES_WIDTH = sum(-(-width // LANES) * LANES for width in SLOPES.values())
 
 
-def backward_kernel(tick, rows, length, hidden, old, count, section, gain_one, gain_two, cosine, sine, *rest):
+def backward_kernel(tick, rows, length, hidden, old, count, saves, section, gain_one, gain_two, cosine, sine, *rest):
     slope_in, rest = rest[:count], rest[count:]
     (wot, wqkvt, wide, tall, stash, sums), rest = rest[:6], rest[6 + old :]
-    entering, leaving, _, _, _, _, made, mixer_out, vot, vqkvt, mixers, sems, mixer_sems = rest
+    entering, leaving, _, _, _, _, made, mixer_out, *far, vot, vqkvt, mixers, sems, mixer_sems, far_sems = rest
+    near = (stash, sums, made)
+    saving = [pltpu.make_async_copy(near[i], far[i], far_sems.at[i]) for i in range(3)] if saves else []
+    for copy in saving[:2]:
+        copy.start()
     width = entering.shape[1]
-    _, _, vdt = wide_views(wide, width)
-    _, vgt, vut, _ = tall_views(tall, hidden, width)
+    if saves:
+        _, _, vdt = halves(wide, width, width, width)
+        _, vgt, vut, _ = halves(tall, hidden, hidden, hidden, width)
+    else:
+        vdt, (vgt, vut) = wide, halves(tall, hidden, hidden)
     piece = hidden // PIECES
 
     @pl.when(section[0] == tick)
@@ -389,34 +394,44 @@
         for write in writes:
             write.wait()
 
-
-def backward_pass(tick, section, slope, gains, tables, stash, streamed, weights, made, mixers, length, hidden, behind):
+    for copy in saving[2:]:
+        copy.start()
+    for copy in saving:
+        copy.wait()
+
+
+def backward_pass(tick, section, slope, gains, tables, stash, streamed, weights, made, mixers, length, hidden, saves):
     rows, width = slope[0].shape[0], weights[1].shape[1]
     held = [*weights, *stash, *made]
     count = len(slope)
     outs = pl.pallas_call(
-        functools.partial(backward_kernel, tick, rows, length, hidden, len(made) + len(mixers) + len(behind), count),
+        functools.partial(backward_kernel, tick, rows, length, hidden, len(made) + len(mixers), count, saves),
         out_shape=[
             jax.ShapeDtypeStruct((rows, width), F32),
             jax.ShapeDtypeStruct((rows, width), BF),
         ]
         + vmem_like([*weights, *stash])
-        + [pltpu.VMEM((2, rows, SLOPES_WIDTH), BF), pltpu.HBM((2, rows, width), BF)],
+        + [pltpu.VMEM((2, rows, SLOPES_WIDTH), BF), pltpu.HBM((2, rows, width), BF)]
+        + (
+            [pltpu.HBM(array.shape, array.dtype) for array in stash] + [pltpu.HBM((2, rows, SLOPES_WIDTH), BF)]
+            if saves
+            else []
+        ),
         in_specs=[pl.BlockSpec(memory_space=pltpu.SMEM)]
         + [vmem()] * (4 + count)
         + [pl.BlockSpec(memory_space=pltpu.HBM)] * 2
         + [vmem()] * len(held)
-        + [pl.BlockSpec(memory_space=pltpu.HBM)] * len(mixers)
-        + [pl.BlockSpec(memory_space=pl.ANY)] * len(behind),
-        out_specs=[vmem()] * 7 + [pl.BlockSpec(memory_space=pltpu.HBM)],
+        + [pl.BlockSpec(memory_space=pltpu.HBM)] * len(mixers),
+        out_specs=[vmem()] * 7 + [pl.BlockSpec(memory_space=pltpu.HBM)] * (4 if saves else 1),
         scratch_shapes=[pltpu.VMEM(w.shape, BF) for w in streamed]
         + [pltpu.VMEM((2, rows, width), BF)]
-        + [pltpu.SemaphoreType.DMA((2,))] * 2,
+        + [pltpu.SemaphoreType.DMA((2,))] * 2
+        + [pltpu.SemaphoreType.DMA((3,))],
         input_output_aliases={7 + count + i: 2 + i for i in range(len(held) + len(mixers))},
         compiler_params=pltpu.CompilerParams(vmem_limit_bytes=16 * MEGA),
         name="backward_pass",
-    )(section, *resident((*gains, *tables, *slope)), *pinned(streamed), *resident(held), *pinned(mixers), *behind)
-    return outs[0], outs[1], outs[2:4], outs[4:6], outs[6:7], outs[7:]
+    )(section, *resident((*gains, *tables, *slope)), *pinned(streamed), *resident(held), *pinned(mixers))
+    return outs[0], outs[1], outs[2:4], outs[4:6], outs[6:7], outs[7:8], outs[8:]
 
 
 def turn(source, target, row=0, column=0):
@@ -428,8 +443,8 @@
 
 def load_kernel(wq, wkt, wvt, wo, wg, wu, wdt, wide, tall, vqkv, wqkvt, sq, vqkvt, sems, out_sem):
     width, pair = wq.shape[0], wkt.shape[0]
-    vg, vu, vdt = wide_views(wide, width)
-    vd, _, _, vo = tall_views(tall, wg.shape[1], width)
+    vg, vu, vdt = halves(wide, width, width, width)
+    vd, _, _, vo = halves(tall, *[wg.shape[1]] * 3, width)
     copies = [
         pltpu.make_async_copy(source, target, sems.at[i])
         for i, (source, target) in enumerate(
@@ -485,32 +500,69 @@
     return weights, joined_back
 
 
-def turn_kernel(hidden, wide, tall, *rest):
-    wot, vot, sem = rest[-3:]
-    width = wot.shape[0]
-    vg, vu, _ = wide_views(wide, width)
-    _, vgt, vut, vo = tall_views(tall, hidden, width)
+def turn_kernel(wide, tall, wide_out, tall_out, wot, wback, vot, sems):
+    hidden, width = wide.shape[1], tall.shape[1]
+    vg, vu, _ = halves(wide, width, width, width)
+    _, vgt, vut, vo = halves(tall, hidden, hidden, hidden, width)
+    copies = [
+        pltpu.make_async_copy(source, target, sems.at[i])
+        for i, (source, target) in enumerate(zip((vot, vgt, vut), [wot] + halves(wback, hidden, hidden)))
+    ]
     vot[:, :width] = vo[...].T
     vot[:, width:] = jnp.zeros((width, HEAD), BF)
-    out = pltpu.make_async_copy(vot, wot, sem)
-    out.start()
-    turn(vg, vgt)
-    turn(vu, vut)
-    out.wait()
+    copies[0].start()
+    for source, target, copy in zip((vg, vu), (vgt, vut), copies[1:]):
+        turn(source, target)
+        copy.start()
+    for copy in copies:
+        copy.wait()
 
 
 def turned(wide, tall):
     hidden, width = wide.shape[1], tall.shape[1]
+    back = (2 * hidden, width)
     return pl.pallas_call(
-        functools.partial(turn_kernel, hidden),
-        out_shape=vmem_like((wide, tall)) + [pltpu.HBM((width, CHUNKS * LANES), BF)],
+        turn_kernel,
+        out_shape=vmem_like((wide, tall))
+        + [pltpu.HBM((width, CHUNKS * LANES), BF), pltpu.HBM(back, BF)],
         in_specs=[vmem()] * 2,
-        out_specs=[vmem()] * 2 + [pl.BlockSpec(memory_space=pltpu.HBM)],
-        scratch_shapes=[pltpu.VMEM((width, CHUNKS * LANES), BF), pltpu.SemaphoreType.DMA],
+        out_specs=[vmem()] * 2 + [pl.BlockSpec(memory_space=pltpu.HBM)] * 2,
+        scratch_shapes=[
+            pltpu.VMEM((width, CHUNKS * LANES), BF),
+            pltpu.SemaphoreType.DMA((3,)),
+        ],
         input_output_aliases={0: 0, 1: 1},
         compiler_params=pltpu.CompilerParams(vmem_limit_bytes=16 * MEGA),
         name="turn_weights",
     )(*resident((wide, tall)))
+
+
+def moved_kernel(count, *refs):
+    copies = [
+        pltpu.make_async_copy(refs[i], refs[count + i], refs[-1].at[i]) for i in range(count)
+    ]
+    for copy in copies:
+        copy.start()
+    for copy in copies:
+        copy.wait()
+
+
+def moved(arrays, inward):
+    count = len(arrays)
+    near, far = (vmem(), pltpu.VMEM), (pl.BlockSpec(memory_space=pltpu.HBM), pltpu.HBM)
+    (source, _), (target, place) = (far, near) if inward else (near, far)
+    return pl.pallas_call(
+        functools.partial(moved_kernel, count),
+        out_shape=[place(array.shape, array.dtype) for array in arrays],
+        in_specs=[source] * count,
+        out_specs=[target] * count,
+        scratch_shapes=[pltpu.SemaphoreType.DMA((count,))],
+        compiler_params=pltpu.CompilerParams(vmem_limit_bytes=16 * MEGA),
+        cost_estimate=pl.CostEstimate(
+            flops=0, bytes_accessed=2 * sum(array.size * array.dtype.itemsize for array in arrays), transcendentals=0
+        ),
+        name="restored" if inward else "saved",
+    )(*(pinned if inward else resident)(arrays))
 
 
 def parts_kernel(normed, context, made, out, stage, sems):
@@ -582,7 +634,7 @@
     return pl.pallas_call(
         factors_kernel,
         grid=(hidden // piece, rows // block),
-        out_shape=[jax.ShapeDtypeStruct((rows, hidden), BF)] * 3,
+        out_shape=[pltpu.HBM((rows, hidden), BF)] * 3,
         in_specs=[
             pl.BlockSpec((block, width), lambda i, j: (j, 0)),
             weight,
@@ -596,41 +648,76 @@
 
 
 def feed_kernel(own, last, mixer, second, chosen, wdt, gate_factor, up_factor, active, *rest):
-    earlier, (gate, up, down, squares) = rest[:-4], rest[-4:]
-    blocks = mixer[...]
-    mine = dot_last(chosen[...], blocks).astype(BF)
-    second_own = dot_last(chosen[...], second[...]).astype(BF)
+    earlier, (gate, up, down, squares, mine, second_own) = rest[:-6], rest[-6:]
+
+    @pl.when(pl.program_id(0) == 0)
+    def pick():
+        mine[...] = dot_last(chosen[...], mixer[...]).astype(BF)
+        second_own[...] = dot_last(chosen[...], second[...]).astype(BF)
+        squares[...] = jnp.zeros_like(squares)
+
+    slope = dot(mixer[...], wdt[...])
+    gate_slope = (slope * gate_factor[...].astype(F32)).astype(BF)
+    up_slope = (slope * up_factor[...].astype(F32)).astype(BF)
+    parts = (dot(second_own[...], gate_slope), dot(second_own[...], up_slope), dot(mine[...], active[...]))
+    for k, (ref, part) in enumerate(zip((gate, up, down), parts)):
+        part = part[:own]
+        if earlier:
+            part = part + earlier[k][...]
+        ref[...] = part
+        if last:
+            squares[...] += jnp.sum(part * part, axis=0, keepdims=True)
+
+
+def feed(own, last, mixer, second, chosen, wdt, made, earlier):
+    rows, width = mixer.shape
+    hidden = wdt.shape[1]
     piece = 512
-    total = None
-    for i in range(wdt.shape[1] // piece):
-        cols = slice(i * piece, (i + 1) * piece)
-        slope = dot(blocks, wdt[:, cols])
-        gate_slope = (slope * gate_factor[:, cols].astype(F32)).astype(BF)
-        up_slope = (slope * up_factor[:, cols].astype(F32)).astype(BF)
-        parts = (dot(second_own, gate_slope), dot(second_own, up_slope), dot(mine, active[:, cols]))
-        for k, (ref, part) in enumerate(zip((gate, up, down), parts)):
-            part = part[:own]
-            if earlier:
-                part = part + earlier[k][:, cols]
-            ref[:, cols] = part
-            if last:
-                square = jnp.sum(part * part, axis=0, keepdims=True)
-                total = square if total is None else total + square
-    squares[...] = total if last else jnp.zeros_like(squares)
-
-
-def feed(own, last, mixer, second, chosen, wdt, made, earlier):
-    hidden = wdt.shape[1]
-    operands = (mixer, second, chosen, wdt, *made, *earlier)
+    whole = lambda i: (0, 0)
+    column = lambda i: (0, i)
+    once = pl.Buffered(1)
+    result = pl.BlockSpec((own, piece), column)
     return pl.pallas_call(
         functools.partial(feed_kernel, own, last),
-        out_shape=[jax.ShapeDtypeStruct((own, hidden), F32)] * 3 + [jax.ShapeDtypeStruct((1, 512), F32)],
-        in_specs=[vmem()] * len(operands),
-        out_specs=[vmem()] * 4,
+        grid=(hidden // piece,),
+        out_shape=[jax.ShapeDtypeStruct((own, hidden), F32)] * 3 + [jax.ShapeDtypeStruct((1, piece), F32)],
+        in_specs=[pl.BlockSpec((rows, width), whole, pipeline_mode=once)] * 2
+        + [pl.BlockSpec(chosen.shape, whole, pipeline_mode=once), pl.BlockSpec((width, piece), column)]
+        + [pl.BlockSpec((rows, piece), column)] * 3
+        + [result] * len(earlier),
+        out_specs=[result] * 3 + [pl.BlockSpec((1, piece), whole)],
+        scratch_shapes=[pltpu.VMEM((chosen.shape[0], rows), BF)] * 2,
         compiler_params=pltpu.CompilerParams(vmem_limit_bytes=16 * MEGA),
-        cost_estimate=pl.CostEstimate(flops=2 * (mixer.shape[0] + 3 * own) * wdt.size, bytes_accessed=8 * mixer.shape[0] * hidden, transcendentals=0),
+        cost_estimate=pl.CostEstimate(
+            flops=2 * (rows + 3 * own) * wdt.size, bytes_accessed=8 * rows * hidden, transcendentals=0
+        ),
         name="feed_gradient",
-    )(*resident(operands))
+    )(mixer, second, chosen, wdt, *made, *earlier)
+
+
+def finish_kernel(terms, squares, query, key, value, output, gains, total):
+    edge = QUERY + 2 * PAIR
+    whole = terms[...].astype(F32)
+    query[...] = whole[:, :QUERY]
+    key[...] = whole[:, QUERY : QUERY + PAIR].T
+    value[...] = whole[:, QUERY + PAIR : edge].T
+    output[...] = whole[:, JOINED : JOINED + QUERY]
+    gains[...] = whole[:, edge : edge + 2]
+    sums = jnp.sum(whole * whole, axis=0, keepdims=True)
+    total[...] = jnp.sum(sums, axis=1, keepdims=True) + jnp.sum(squares[...], axis=1, keepdims=True)
+
+
+def finish(terms, squares):
+    own = terms.shape[0]
+    shapes = ((own, QUERY), (PAIR, own), (PAIR, own), (own, QUERY), (own, 2), (1, 1))
+    return pl.pallas_call(
+        finish_kernel,
+        out_shape=[jax.ShapeDtypeStruct(shape, F32) for shape in shapes],
+        in_specs=[vmem()] * 2,
+        out_specs=[vmem()] * len(shapes),
+        compiler_params=pltpu.CompilerParams(vmem_limit_bytes=16 * MEGA),
+        name="finish",
+    )(terms, squares)
 
 
 def after(value, *tokens):
@@ -682,12 +769,12 @@
         return [half[band] for half in (mine, other) for band in bands]
 
 
-def summed(value, axis):
-    count, distance = lax.axis_size(axis), 1
-    while distance < count:
-        value = value + lax.ppermute(value, axis, [(i, i ^ distance) for i in range(count)])
-        distance *= 2
-    return value
+def summed(value, axis, distances):
+    count = lax.axis_size(axis)
+    values = [value] + [lax.ppermute(value, axis, [(i, i ^ d) for i in range(count)]) for d in distances]
+    while len(values) > 1:
+        values = [a + b for a, b in zip(values[::2], values[1::2])]
+    return values[0]
 
 
 def per_device(
@@ -725,17 +812,17 @@
         if t < sections - 1:
             x = [lax.ppermute(leaving, "section", [(t, t + 1)])]
         if t == 0:
-            *changed, output_back = turned(*weights[:2])
-            weights = [*changed, weights[2]]
+            *changed, output_back, back_far = turned(*weights[:2])
+            weights = [*changed, *weights[2:]]
     normed, context, second = lefts
     streamed = (output_back, joined_back)
     weights = weights[:2]
 
     slope = last_slope
-    made = mixers = behind = ()
+    made = mixers = ()
     for t in reversed(range(sections)):
-        entering, leaving, weights, stash, made, mixers = backward_pass(
-            t, place, slope, gains, tables, stash, streamed, weights, made, mixers, length, hidden, behind
+        entering, leaving, weights, stash, made, mixers, far = backward_pass(
+            t, place, slope, gains, tables, stash, streamed, weights, made, mixers, length, hidden, t == sections - 1
         )
         if t > 0:
             slope = [lax.ppermute(leaving, "section", [(t, t - 1)])]
@@ -743,7 +830,9 @@
             outputs = spread_from(after(final, leaving).astype(BF), "section", sections - 1)
         if t > 0:
             if t == sections - 1:
-                second_all = lax.all_gather(after(second.reshape(2 * rows, width), leaving), "dp", axis=0, tiled=True)
+                second_all = lax.all_gather(after(second.reshape(2 * rows, width), far[0]), "dp", axis=0, tiled=True)
+                near = moved((w_down, back_far, *far), True)
+                weights, stash, made = near[:2], near[2:4], near[4:]
     slopes = made
     bands = [slice(start, start + BAND) for start in range(0, 2 * rows * replicas, BAND)]
     second_all = [second_all[band] for band in bands]
@@ -751,25 +840,26 @@
     mixer_all = [mixer_all[band] for band in bands]
     delta_inputs = spread_from(leaving, "section", 0)
     terms = parts(normed, context, slopes[0])
-    reduced = lax.psum_scatter(terms, "dp", scatter_dimension=0, tiled=True).astype(F32)
+    reduced = lax.psum_scatter(terms, "dp", scatter_dimension=0, tiled=True)
     made = [factors(second, w_gate, w_up) for second in second_all]
     feed_parts = ()
     for i, (mixer, second, item) in enumerate(zip(mixer_all, second_all, made)):
         last = i == len(made) - 1
         *feed_parts, squares = feed(own, last, mixer, second, chosen, w_down, item, feed_parts)
     gate, up, down = feed_parts
-    total = jnp.sum(squares) + jnp.sum(reduced * reduced)
-    total = summed(summed(total.reshape(1), "dp"), "section")
-    edge = QUERY + 2 * PAIR
+    query, key, value, output, gain_terms, total = finish(reduced, squares)
+    total = summed(total, "dp", [1])
+    total = summed(total, "dp", range(2, replicas, 2))
+    total = summed(total, "section", range(1, sections))
     return (
         outputs.astype(F32).reshape(micro, length, part),
         delta_inputs.astype(F32).reshape(micro, length, part),
-        reduced[:, edge][None],
-        reduced[:, :QUERY][None],
-        reduced[:, QUERY : QUERY + PAIR][None],
-        reduced[:, QUERY + PAIR : edge][None],
-        reduced[:, JOINED : JOINED + QUERY][None],
-        reduced[:, edge + 1][None],
+        gain_terms[:, 0][None],
+        query[None],
+        key.T[None],
+        value.T[None],
+        output[None],
+        gain_terms[:, 1][None],
         gate[None],
         up[None],
         down.T[None],

time: 360 us -> 317 us (0.88)
  local copies, waits for them, and re-layouts: 81.9 us -> 30.5 us
  Pallas kernels: 114 us -> 133 us
  waiting for transfers between devices: 98.1 us -> 89.8 us
    unnamed x94 -> x60, local copies, waits for them, and re-layouts: 74.2 us -> 24 us
    pallas_call x3 -> x5, Pallas kernels: 25.8 us -> 42 us  [the longest x2 26.4 us: feed(): pl.pallas_call(functools.partial(feed_kernel, own, last), grid=(hidden //...]
    ppermute x3, waiting for transfers between devices: 90.5 us -> 81.1 us  [per_device(): slope = [lax.ppermute(leaving, 'section', [(t, t - 1)])]]
    unnamed x4, waiting for transfers between devices: 0.05 us -> 4.07 us
    ppermute x5 -> x7, starting transfers between devices: 13 us -> 14.9 us  [summed(): lax.ppermute(value, axis, [(i, i ^ d) for i in range(count)])]
  transfers between devices with their start and end apart: 26 -> 28, of which waited for: 8 -> 7; matrix products, arithmetic and copies ran while one was open for 2% -> 3% of each run, Pallas kernels for 26% -> 34%
where the time goes in v2:
time: 317 us; the launch traced here: 313 us
  Pallas kernels  133 us (42%)
  waiting for transfers between devices  89.8 us (28%)
  starting transfers between devices  36.7 us (12%)
  local copies, waits for them, and re-layouts  30.5 us (10%)
  between operations  21.1 us (7%)
    ppermute x3, waiting for transfers between devices, per_device(): slope = [lax.ppermute(leaving, 'section', [(t, t - 1)])]  81.1 us
    pallas_call x2, Pallas kernels, factors(): pl.pallas_call(factors_kernel, grid=(hidden // piece, rows // block), out...  31 us
    pallas_call x4, Pallas kernels, backward_pass(): pl.pallas_call(functools.partial(backward_kernel, tick, rows, length, hid...  30 us
    pallas_call x2, Pallas kernels, feed(): pl.pallas_call(functools.partial(feed_kernel, own, last), grid=(hidden //...  26.4 us
    unnamed x60, local copies, waits for them, and re-layouts  24 us
    pallas_call x4, Pallas kernels, forward_pass(): pl.pallas_call(functools.partial(forward_kernel, tick, rows, length, hidd...  18.1 us
    ppermute x7, starting transfers between devices, summed(): lax.ppermute(value, axis, [(i, i ^ d) for i in range(count)])  14.9 us
    ppermute x6, starting transfers between devices, spread_from(): mine = mine + lax.ppermute(columns[s], axis, [(source, s)])  9.65 us
  transfers between devices with their start and end apart: 28, of which 7 were waited for; matrix products, arithmetic and copies ran while one was open for 3% of the time, Pallas kernels for 34%

profile of v2, /device:TPU:0, one launch (start us, length us, event | category | flops | bytes accessed | tf_op | source)
XLA Modules:
  0.0 313.3 jit_solution(3335992614062090525)
XLA Ops:
  7.2 1.3 collective-permute-start
  8.5 1.3 collective-permute-start.1
  9.8 1.3 collective-permute-start.2
  11.2 8.1 %load_weights.1 = (bf16[2880,2560]{1,0:T(8,128)(2,1)S(1)}, bf16[8640,960]{1,0:T(8,128)(2,1)S(1)}, bf16[960,1664]{1,0:T(8,128)(2,1)S(1)}, bf16[1664,960]{1,0:T(8,128)(2,1)}) custom-call(bf16[960,960]{1,0:T(8,128)(2,1)} %bitcast.61, bf16[320,960]{1,0:T(8,128)(2,1)} %bitcast.63, bf16[320,960]{1,0:T(8,128)(2,1)} %bitcast.64, bf16[960,960]{1,0:T(8,128)(2,1)} %bitcast.62, ...), custom_call_target="tpu_custom_call" | custom-call | tf_op jit(solution)/shard_map/load_weights/pallas_call | solution.py:481
  19.4 12.4 %forward_pass.4 = (f32[128,960]{1,0:T(8,128)}, bf16[128,960]{1,0:T(8,128)(2,1)}, bf16[2880,2560]{1,0:T(8,128)(2,1)S(1)}, bf16[8640,960]{1,0:T(8,128)(2,1)S(1)}, ...) custom-call(s32[1]{0:T(128)} %bitcast.1.section, ...), custom_call_target="tpu_custom_call", output_to_operand_aliasing={{2}: (9, {}), {3}: (10, {}), {4}: (11, {})} | custom-call | tf_op jit(solution)/shard_map/forward_pass/pallas_call | solution.py:245
  31.8 1.5 collective-permute-start.3
  33.4 6.1 %turn_weights.1 = (bf16[2880,2560]{1,0:T(8,128)(2,1)S(1)}, bf16[8640,960]{1,0:T(8,128)(2,1)S(1)}, bf16[960,1024]{1,0:T(8,128)(2,1)}, bf16[5120,960]{1,0:T(8,128)(2,1)}) custom-call(bf16[2880,2560]{1,0:T(8,128)(2,1)S(1)} %get-tuple-element.111.wide, bf16[8640,960]{1,0:T(8,128)(2,1)S(1)} %get-tuple-element.112.tall), custom_call_target="tpu_custom_call", output_to_operand_aliasing={{0}: (0, {}), {1}: (1, {})} | custom-call | tf_op jit(solution)/shard_map/turn_weights/pallas_call | solution.py:524
  41.5 1.4 forward_pass.6
  43.6 1.3 collective-permute-start.6
  46.3 3.4 %forward_pass.7 = (f32[128,960]{1,0:T(8,128)}, bf16[128,960]{1,0:T(8,128)(2,1)}, bf16[2880,2560]{1,0:T(8,128)(2,1)S(1)}, bf16[8640,960]{1,0:T(8,128)(2,1)S(1)}, ...) custom-call(s32[1]{0:T(128)} %bitcast.1.section, ...), custom_call_target="tpu_custom_call", output_to_operand_aliasing={{2}: (6, {}), {3}: (7, {}), {4}: (8, {}), {5}: (9, {}), {6}... | custom-call | tf_op jit(solution)/shard_map/forward_pass/pallas_call | solution.py:245
  49.7 9.4 %backward_pass.4 = (f32[128,960]{1,0:T(8,128)}, bf16[128,960]{1,0:T(8,128)(2,1)}, bf16[2880,2560]{1,0:T(8,128)(2,1)S(1)}, bf16[8640,960]{1,0:T(8,128)(2,1)S(1)},...) custom-call(s32[1]{0:T(128)} %bitcast.1.section, ...), custom_call_target="tpu_custom_call", output_to_operand_aliasing={{2}: (11, {}), {3}: (12, {}), {4}: (13, {}), {5}: (14, {})} | custom-call | tf_op jit(solution)/shard_map/backward_pass/pallas_call | solution.py:407
  59.8 8.4 %restored.1 = (bf16[960,2560]{1,0:T(8,128)(2,1)S(1)}, bf16[5120,960]{1,0:T(8,128)(2,1)S(1)}, bf16[2,128,10752]{2,1,0:T(8,128)(2,1)S(1)}, f32[2,2,128,960]{3,2,1,0:T(8,128)S(1)}, bf16[2,128,4736]{2,1,0:T(8,128)(2,1)S(1)}) custom-call(bf16[960,2560]{1,0:T(8,128)(2,1)} %bitcast.40, bf16[5120,960]{1,0:T(8,128)(2,1)} %get-tuple-element.148.refs_1_, ...), custom_call_target="tpu_custom_call" | custom-call | bytes 49283072 | tf_op jit(solution)/shard_map/restored/pallas_call | solution.py:554
  68.2 1.3 backward_pass.5
  70.2 6.3 %backward_pass.6 = (f32[128,960]{1,0:T(8,128)}, bf16[128,960]{1,0:T(8,128)(2,1)S(1)}, bf16[960,2560]{1,0:T(8,128)(2,1)S(1)}, bf16[5120,960]{1,0:T(8,128)(2,1)S(1...) custom-call(s32[1]{0:T(128)} %bitcast.1.section, ...), custom_call_target="tpu_custom_call", output_to_operand_aliasing={{2}: (8, {}), {3}: (9, {}), {4}: (10, {}), {5}: (11, {}), {... | custom-call | tf_op jit(solution)/shard_map/backward_pass/pallas_call | solution.py:407
  76.5 1.3 collective-permute-start.14
  77.8 81.1 %collective-permute-done.14.rest_0_ = bf16[128,960]{1,0:T(8,128)(2,1)S(1)} collective-permute-done((bf16[128,960]{1,0:T(8,128)(2,1)S(1)}, bf16[128,960]{1,0:T(8,128)(2,1)S(1)}, u32[]{:S(2)}, u32[]{:S(2)}) %collective-permute-start.14) | collective-permute-done | bytes 245792 | tf_op jit(solution)/shard_map/ppermute | solution.py:828
  158.9 13.1 %backward_pass.7 = (f32[128,960]{1,0:T(8,128)}, bf16[128,960]{1,0:T(8,128)(2,1)S(1)}, bf16[960,2560]{1,0:T(8,128)(2,1)S(1)}, bf16[5120,960]{1,0:T(8,128)(2,1)S(1...) custom-call(s32[1]{0:T(128)} %bitcast.1.section, ...), custom_call_target="tpu_custom_call", output_to_operand_aliasing={{2}: (8, {}), {3}: (9, {}), {4}: (10, {}), {5}: (11, {}), {... | custom-call | tf_op jit(solution)/shard_map/backward_pass/pallas_call | solution.py:407
  172.8 3.6 %attention_parts.1 = bf16[960,2688]{1,0:T(8,128)(2,1)} custom-call(bf16[2,128,960]{2,1,0:T(8,128)(2,1)S(1)} %copy-done.5, bf16[2,128,960]{2,1,0:T(8,128)(2,1)S(1)} %copy-done.6, bf16[2,128,4736]{2,1,0:T(8,128)(2,1)S(1)} %get-tuple-element.175.made), custom_call_target="tpu_custom_call" | custom-call | flops 2642411520 | bytes 10321920 | tf_op jit(solution)/shard_map/attention_parts/pallas_call | solution.py:602
  179.0 1.5 collective-permute-start.9
  180.7 1.3 collective-permute-start.15
  182.0 1.3 collective-permute-start.16
  183.3 4.2 %collective-permute-start.17 = (bf16[128,240]{1,0:T(8,128)(2,1)S(1)}, bf16[128,240]{1,0:T(8,128)(2,1)S(1)}, u32[]{:S(2)}, u32[]{:S(2)}) collective-permute-start(bf16[128,240]{1,0:T(8,128)(2,1)S(1)} %get-tuple-element.205), channel_id=1, source_target_pairs={{0,24},{1,25},{2,26},{3,27},{4,28},{5,29},{6,30},{7,31}} | collective-permute-start | bytes 184328 | tf_op jit(solution)/shard_map/ppermute | solution.py:740
  188.3 1.1 collective-permute-done.17
  190.1 2.7 fusion.5
  192.8 3.2 %copy-done.3 = bf16[1,960,2560]{2,1,0:T(8,128)(2,1)S(1)} copy-done((bf16[1,960,2560]{2,1,0:T(8,128)(2,1)S(1)}, bf16[1,960,2560]{2,1,0:T(8,128)(2,1)}, u32[]{:S(2)}) %copy-start.3) | copy-done | bytes 4915224
  196.0 2.4 copy-done.4
  198.4 15.6 %feed_factors.3 = (bf16[1024,2560]{1,0:T(8,128)(2,1)}, bf16[1024,2560]{1,0:T(8,128)(2,1)}, bf16[1024,2560]{1,0:T(8,128)(2,1)}) custom-call(bf16[1024,960]{1,0:T(8,128)(2,1)S(1)} %get-tuple-element.200.second, bf16[960,2560]{1,0:T(8,128)(2,1)S(1)} %bitcast.46, bf16[960,2560]{1,0:T(8,128)(2,1)S(1)} %bitcast.49), custom_call_target="tpu_custom_call" | custom-call | flops 10066329600 | bytes 20971520 | tf_op jit(solution)/shard_map/feed_factors/pallas_call | solution.py:634
  214.0 15.4 %feed_factors.2 = (bf16[1024,2560]{1,0:T(8,128)(2,1)}, bf16[1024,2560]{1,0:T(8,128)(2,1)}, bf16[1024,2560]{1,0:T(8,128)(2,1)}) custom-call(bf16[1024,960]{1,0:T(8,128)(2,1)S(1)} %get-tuple-element.201.second, bf16[960,2560]{1,0:T(8,128)(2,1)S(1)} %bitcast.47, bf16[960,2560]{1,0:T(8,128)(2,1)S(1)} %bitcast.50), custom_call_target="tpu_custom_call" | custom-call | flops 10066329600 | bytes 20971520 | tf_op jit(solution)/shard_map/feed_factors/pallas_call | solution.py:634
  229.4 2.8 fusion.6
  232.3 2.5 copy-done
  234.8 1.6 copy-done.11
  236.4 2.6 copy-done.24
  239.0 2.6 copy-done.25
  241.5 2.6 copy-done.26
  244.1 12.9 %feed_gradient.2 = (f32[120,2560]{1,0:T(8,128)S(1)}, f32[120,2560]{1,0:T(8,128)S(1)}, f32[120,2560]{1,0:T(8,128)S(1)}, f32[1,512]{1,0:T(1,128)}) custom-call(bf16[1024,960]{1,0:T(8,128)(2,1)S(1)} %get-tuple-element.202.mixer, bf16[1024,960]{1,0:T(8,128)(2,1)S(1)} %copy-done.11, bf16[128,960]{1,0:T(8,128)(2,1)S(1)} %copy-done.16, ...), custom_call_target="tpu_custom_call" | custom-call | flops 6802636800 | bytes 20971520 | tf_op jit(solution)/shard_map/feed_gradient/pallas_call | solution.py:680
  259.1 1.3 copy-done.13
  260.4 1.3 copy-done.15
  261.7 13.5 %feed_gradient.3 = (f32[120,2560]{1,0:T(8,128)}, f32[120,2560]{1,0:T(8,128)}, f32[120,2560]{1,0:T(8,128)}, f32[1,512]{1,0:T(1,128)S(1)}) custom-call(bf16[1024,960]{1,0:T(8,128)(2,1)S(1)} %get-tuple-element.203.mixer, bf16[1024,960]{1,0:T(8,128)(2,1)S(1)} %get-tuple-element.201.second, bf16[128,960]{1,0:T(8,128)(2,1)S(1)} %copy-done.16, ...), custom_call_target="tpu_custom_call" | custom-call | flops 6802636800 | bytes 20971520 | tf_op jit(solution)/shard_map/feed_gradient/pallas_call | solution.py:680
  275.2 4.0 %reduce-scatter.4.cloned.1.call-done.terms = bf16[120,2688]{1,0:T(8,128)(2,1)} async-done(((bf16[960,2688]{1,0:T(8,128)(2,1)}), bf16[120,2688]{1,0:T(8,128)(2,1)}) %reduce-scatter.4.cloned.1.call-update) | async-done | bytes 645136
  279.2 1.1 copy-done.17
  280.3 1.1 finish.1
  284.0 1.7 collective-permute-start.20
  285.7 2.8 collective-permute-start.21
  288.5 2.9 collective-permute-start.19
  294.1 2.8 collective-permute-start.23
  296.9 2.8 collective-permute-start.24
  299.7 1.9 collective-permute-start.22
  301.6 1.8 collective-permute-done.22
  (102 shorter events, 14.4 us)
Async XLA Ops:
  7.2 182.9 %all-gather.5.cloned.1.call-start = ((), (), s32[]{:S(2)}) async-start(), calls=%async_computation.2 | async-start | bytes 4718592 | tf_op jit(solution)/shard_map/all_gather | solution.py:833
  7.2 12.1 %collective-permute-start = (bf16[128,240]{1,0:T(8,128)(2,1)}, bf16[128,240]{1,0:T(8,128)(2,1)S(1)}, u32[]{:S(2)}, u32[]{:S(2)}) collective-permute-start(bf16[128,240]{1,0:T(8,128)(2,1)} %bitcast.51), channel_id=1, source_target_pairs={{8,0},{9,1},{10,2},{11,3},{12,4},{13,5},{14,6},{15,7}} | collective-permute-start | bytes 184328 | tf_op jit(solution)/shard_map/ppermute | solution.py:729
  8.5 10.8 %collective-permute-start.1 = (bf16[128,240]{1,0:T(8,128)(2,1)}, bf16[128,240]{1,0:T(8,128)(2,1)S(1)}, u32[]{:S(2)}, u32[]{:S(2)}) collective-permute-start(bf16[128,240]{1,0:T(8,128)(2,1)} %bitcast.52), channel_id=1, source_target_pairs={{16,0},{17,1},{18,2},{19,3},{20,4},{21,5},{22,6},{23,7}} | collective-permute-start | bytes 184328 | tf_op jit(solution)/shard_map/ppermute | solution.py:729
  9.8 9.5 %collective-permute-start.2 = (bf16[128,240]{1,0:T(8,128)(2,1)}, bf16[128,240]{1,0:T(8,128)(2,1)S(1)}, u32[]{:S(2)}, u32[]{:S(2)}) collective-permute-start(bf16[128,240]{1,0:T(8,128)(2,1)} %bitcast.53), channel_id=1, source_target_pairs={{24,0},{25,1},{26,2},{27,3},{28,4},{29,5},{30,6},{31,7}} | collective-permute-start | bytes 184328 | tf_op jit(solution)/shard_map/ppermute | solution.py:729
  11.1 8.2 %copy-start.7 = (f32[128,128]{1,0:T(8,128)S(1)}, f32[128,128]{1,0:T(8,128)}, u32[]{:S(2)}) copy-start(f32[128,128]{1,0:T(8,128)} %constant.21.clone.cosine) | copy-start | bytes 196612
  11.1 8.2 %copy-start.8 = (f32[128,128]{1,0:T(8,128)S(1)}, f32[128,128]{1,0:T(8,128)}, u32[]{:S(2)}) copy-start(f32[128,128]{1,0:T(8,128)} %constant.22.clone.sine) | copy-start | bytes 196612
  11.2 8.2 %copy-start.20 = (f32[1,960]{1,0:T(1,128)S(1)}, f32[1,960]{1,0:T(1,128)}, u32[]{:S(2)}) copy-start(f32[1,960]{1,0:T(1,128)} %gain_one.15) | copy-start | bytes 11524
  11.2 8.2 %copy-start.21 = (f32[1,960]{1,0:T(1,128)S(1)}, f32[1,960]{1,0:T(1,128)}, u32[]{:S(2)}) copy-start(f32[1,960]{1,0:T(1,128)} %gain_two.15) | copy-start | bytes 11524
  11.2 8.2 %copy-start.22 = (bf16[4,32,240]{2,1,0:T(8,128)(2,1)S(1)}, bf16[4,32,240]{2,1,0:T(8,128)(2,1)}, u32[]{:S(2)}) copy-start(bf16[4,32,240]{2,1,0:T(8,128)(2,1)} %param.13) | copy-start | bytes 184324
  31.8 8.1 %collective-permute-start.3 = (bf16[128,960]{1,0:T(8,128)(2,1)}, bf16[128,960]{1,0:T(8,128)(2,1)S(1)}, u32[]{:S(2)}, u32[]{:S(2)}) collective-permute-start(bf16[128,960]{1,0:T(8,128)(2,1)} %get-tuple-element.110), channel_id=1, source_target_pairs={{0,8},{1,9},{2,10},{3,11},{4,12},{5,13},{6,14},{7,15}} | collective-permute-start | bytes 737288 | tf_op jit(solution)/shard_map/ppermute | solution.py:813
  40.8 0.7 collective-permute-start.4
  42.9 3.3 %collective-permute-start.5 = (bf16[128,960]{1,0:T(8,128)(2,1)}, bf16[128,960]{1,0:T(8,128)(2,1)S(1)}, u32[]{:S(2)}, u32[]{:S(2)}) collective-permute-start(bf16[128,960]{1,0:T(8,128)(2,1)} %get-tuple-element.130), channel_id=1, source_target_pairs={{16,24},{17,25},{18,26},{19,27},{20,28},{21,29},{22,30},{23,31}} | collective-permute-start | bytes 737288 | tf_op jit(solution)/shard_map/ppermute | solution.py:813
  43.6 6.0 %collective-permute-start.6 = (bf16[128,240]{1,0:T(8,128)(2,1)S(1)}, bf16[128,240]{1,0:T(8,128)(2,1)S(1)}, u32[]{:S(2)}, u32[]{:S(2)}) collective-permute-start(bf16[128,240]{1,0:T(8,128)(2,1)S(1)} %bitcast.55), channel_id=1, source_target_pairs={{0,24},{1,25},{2,26},{3,27},{4,28},{5,29},{6,30},{7,31}} | collective-permute-start | bytes 184328 | tf_op jit(solution)/shard_map/ppermute | solution.py:729
  44.9 4.7 %collective-permute-start.7 = (bf16[128,240]{1,0:T(8,128)(2,1)S(1)}, bf16[128,240]{1,0:T(8,128)(2,1)S(1)}, u32[]{:S(2)}, u32[]{:S(2)}) collective-permute-start(bf16[128,240]{1,0:T(8,128)(2,1)S(1)} %bitcast.56), channel_id=1, source_target_pairs={{8,24},{9,25},{10,26},{11,27},{12,28},{13,29},{14,30},{15,31}} | collective-permute-start | bytes 184328 | tf_op jit(solution)/shard_map/ppermute | solution.py:729
  45.6 4.1 %collective-permute-start.8 = (bf16[128,240]{1,0:T(8,128)(2,1)S(1)}, bf16[128,240]{1,0:T(8,128)(2,1)S(1)}, u32[]{:S(2)}, u32[]{:S(2)}) collective-permute-start(bf16[128,240]{1,0:T(8,128)(2,1)S(1)} %bitcast.57), channel_id=1, source_target_pairs={{16,24},{17,25},{18,26},{19,27},{20,28},{21,29},{22,30},{23,31}} | collective-permute-start | bytes 184328 | tf_op jit(solution)/shard_map/ppermute | solution.py:729
  59.1 170.3 %all-gather.3.cloned.1.call-start = ((), (), s32[]{:S(2)}) async-start(), calls=%async_computation.1 | async-start | bytes 4718592 | tf_op jit(solution)/shard_map/all_gather | solution.py:839
  59.1 9.1 %collective-permute-start.12 = (bf16[128,960]{1,0:T(8,128)(2,1)}, bf16[128,960]{1,0:T(8,128)(2,1)S(1)}, u32[]{:S(2)}, u32[]{:S(2)}) collective-permute-start(bf16[128,960]{1,0:T(8,128)(2,1)} %get-tuple-element.146), channel_id=1, source_target_pairs={{24,16},{25,17},{26,18},{27,19},{28,20},{29,21},{30,22},{31,23}} | collective-permute-start | bytes 737288 | tf_op jit(solution)/shard_map/ppermute | solution.py:828
  69.5 0.7 collective-permute-start.13
  70.2 88.7 %copy-start.9 = (f32[128,128]{1,0:T(8,128)S(1)}, f32[128,128]{1,0:T(8,128)}, u32[]{:S(2)}) copy-start(f32[128,128]{1,0:T(8,128)} %constant.22.clone.sine) | copy-start | bytes 196612
  76.5 82.4 %collective-permute-start.14 = (bf16[128,960]{1,0:T(8,128)(2,1)S(1)}, bf16[128,960]{1,0:T(8,128)(2,1)S(1)}, u32[]{:S(2)}, u32[]{:S(2)}) collective-permute-start(bf16[128,960]{1,0:T(8,128)(2,1)S(1)} %get-tuple-element.165), channel_id=1, source_target_pairs={{8,0},{9,1},{10,2},{11,3},{12,4},{13,5},{14,6},{15,7}} | collective-permute-start | bytes 737288 | tf_op jit(solution)/shard_map/ppermute | solution.py:828
  158.9 13.9 %copy-start.5 = (bf16[2,128,960]{2,1,0:T(8,128)(2,1)S(1)}, bf16[2,128,960]{2,1,0:T(8,128)(2,1)}, u32[]{:S(2)}) copy-start(bf16[2,128,960]{2,1,0:T(8,128)(2,1)} %get-tuple-element.173.normed) | copy-start | bytes 1474564
  158.9 13.9 %copy-start.6 = (bf16[2,128,960]{2,1,0:T(8,128)(2,1)S(1)}, bf16[2,128,960]{2,1,0:T(8,128)(2,1)}, u32[]{:S(2)}) copy-start(bf16[2,128,960]{2,1,0:T(8,128)(2,1)} %get-tuple-element.174.context) | copy-start | bytes 1474564
  172.8 106.5 %reduce-scatter.4.cloned.1.call-start = ((), (), s32[]{:S(2)}) async-start(), calls=%async_computation.3 | async-start | bytes 5806080
  176.5 4.1 %copy-start.19 = (bf16[128,960]{1,0:T(8,128)(2,1)S(1)}, bf16[128,960]{1,0:T(8,128)(2,1)}, u32[]{:S(2)}) copy-start(bf16[128,960]{1,0:T(8,128)(2,1)} %copy-done.18) | copy-start | bytes 737284
  177.7 5.6 %collective-permute-start.10 = (bf16[128,240]{1,0:T(8,128)(2,1)S(1)}, bf16[128,240]{1,0:T(8,128)(2,1)S(1)}, u32[]{:S(2)}, u32[]{:S(2)}) collective-permute-start(bf16[128,240]{1,0:T(8,128)(2,1)S(1)} %get-tuple-element.209), channel_id=1, source_target_pairs={{24,8},{25,9},{26,10},{27,11},{28,12},{29,13},{30,14},{31,15}} | collective-permute-start | bytes 184328 | tf_op jit(solution)/shard_map/ppermute | solution.py:740
  178.3 9.2 %collective-permute-start.11 = (bf16[128,240]{1,0:T(8,128)(2,1)S(1)}, bf16[128,240]{1,0:T(8,128)(2,1)S(1)}, u32[]{:S(2)}, u32[]{:S(2)}) collective-permute-start(bf16[128,240]{1,0:T(8,128)(2,1)S(1)} %get-tuple-element.208), channel_id=1, source_target_pairs={{24,16},{25,17},{26,18},{27,19},{28,20},{29,21},{30,22},{31,23}} | collective-permute-start | bytes 184328 | tf_op jit(solution)/shard_map/ppermute | solution.py:740
  179.0 8.5 %collective-permute-start.9 = (bf16[128,240]{1,0:T(8,128)(2,1)S(1)}, bf16[128,240]{1,0:T(8,128)(2,1)S(1)}, u32[]{:S(2)}, u32[]{:S(2)}) collective-permute-start(bf16[128,240]{1,0:T(8,128)(2,1)S(1)} %get-tuple-element.207), channel_id=1, source_target_pairs={{24,0},{25,1},{26,2},{27,3},{28,4},{29,5},{30,6},{31,7}} | collective-permute-start | bytes 184328 | tf_op jit(solution)/shard_map/ppermute | solution.py:740
  180.7 7.6 %collective-permute-start.15 = (bf16[128,240]{1,0:T(8,128)(2,1)S(1)}, bf16[128,240]{1,0:T(8,128)(2,1)S(1)}, u32[]{:S(2)}, u32[]{:S(2)}) collective-permute-start(bf16[128,240]{1,0:T(8,128)(2,1)S(1)} %get-tuple-element.204), channel_id=1, source_target_pairs={{0,8},{1,9},{2,10},{3,11},{4,12},{5,13},{6,14},{7,15}} | collective-permute-start | bytes 184328 | tf_op jit(solution)/shard_map/ppermute | solution.py:740
  182.0 6.3 %collective-permute-start.16 = (bf16[128,240]{1,0:T(8,128)(2,1)S(1)}, bf16[128,240]{1,0:T(8,128)(2,1)S(1)}, u32[]{:S(2)}, u32[]{:S(2)}) collective-permute-start(bf16[128,240]{1,0:T(8,128)(2,1)S(1)} %get-tuple-element.206), channel_id=1, source_target_pairs={{0,16},{1,17},{2,18},{3,19},{4,20},{5,21},{6,22},{7,23}} | collective-permute-start | bytes 184328 | tf_op jit(solution)/shard_map/ppermute | solution.py:740
  183.3 6.1 %collective-permute-start.17 = (bf16[128,240]{1,0:T(8,128)(2,1)S(1)}, bf16[128,240]{1,0:T(8,128)(2,1)S(1)}, u32[]{:S(2)}, u32[]{:S(2)}) collective-permute-start(bf16[128,240]{1,0:T(8,128)(2,1)S(1)} %get-tuple-element.205), channel_id=1, source_target_pairs={{0,24},{1,25},{2,26},{3,27},{4,28},{5,29},{6,30},{7,31}} | collective-permute-start | bytes 184328 | tf_op jit(solution)/shard_map/ppermute | solution.py:740
  192.8 21.2 %copy-start.10 = (bf16[1024,960]{1,0:T(8,128)(2,1)}, bf16[1024,960]{1,0:T(8,128)(2,1)S(1)}, u32[]{:S(2)}) copy-start(bf16[1024,960]{1,0:T(8,128)(2,1)S(1)} %get-tuple-element.200.second) | copy-start | bytes 5898244
  192.8 3.2 %copy-start.3 = (bf16[1,960,2560]{2,1,0:T(8,128)(2,1)S(1)}, bf16[1,960,2560]{2,1,0:T(8,128)(2,1)}, u32[]{:S(2)}) copy-start(bf16[1,960,2560]{2,1,0:T(8,128)(2,1)} %param.21) | copy-start | bytes 14745604
  229.4 2.9 copy-start.16
  229.4 29.6 %slice-start = ((s8[5242880]{0:T(1024)(128)(4,1)}), s8[4194304]{0:T(1024)(128)(4,1)S(1)}, s32[]{:S(2)}) async-start(s8[5242880]{0:T(1024)(128)(4,1)} %bitcast.43), calls=%async_computation.4 | async-start | bytes 8388608
  232.3 2.5 copy-start
  236.4 2.6 copy-start.24
  239.0 2.6 copy-start.25
  241.5 2.6 copy-start.26
  244.1 15.0 %slice-start.1 = ((s8[5242880]{0:T(1024)(128)(4,1)}), s8[1048576]{0:T(1024)(128)(4,1)S(1)}, s32[]{:S(2)}) async-start(s8[5242880]{0:T(1024)(128)(4,1)} %bitcast.43), calls=%async_computation.5 | async-start | bytes 2097152
  244.1 15.0 %copy-start.1 = (bf16[1024,2560]{1,0:T(8,128)(2,1)S(1)}, bf16[1024,2560]{1,0:T(8,128)(2,1)}, u32[]{:S(2)}) copy-start(bf16[1024,2560]{1,0:T(8,128)(2,1)} %get-tuple-element.180.up_factor) | copy-start | bytes 15728644
  244.1 15.0 %copy-start.2 = (bf16[1024,2560]{1,0:T(8,128)(2,1)S(1)}, bf16[1024,2560]{1,0:T(8,128)(2,1)}, u32[]{:S(2)}) copy-start(bf16[1024,2560]{1,0:T(8,128)(2,1)} %get-tuple-element.181.active) | copy-start | bytes 15728644
  281.4 1.2 collective-permute-start.18
  284.0 8.8 %collective-permute-start.20 = (f32[1,1]{1,0:T(1,128)}, f32[1,1]{1,0:T(1,128)}, u32[]{:S(2)}, u32[]{:S(2)}) collective-permute-start(f32[1,1]{1,0:T(1,128)} %add.56), channel_id=1, source_target_pairs={{0,4},{1,5},{2,6},{3,7},{4,0},{5,1},{6,2},{7,3},{8,12},{9,13},{10,... | collective-permute-start | bytes 20 | tf_op jit(solution)/shard_map/ppermute | solution.py:774
  285.7 7.1 %collective-permute-start.21 = (f32[1,1]{1,0:T(1,128)}, f32[1,1]{1,0:T(1,128)}, u32[]{:S(2)}, u32[]{:S(2)}) collective-permute-start(f32[1,1]{1,0:T(1,128)} %add.56), channel_id=1, source_target_pairs={{0,6},{1,7},{2,4},{3,5},{4,2},{5,3},{6,0},{7,1},{8,14},{9,15},{10,... | collective-permute-start | bytes 20 | tf_op jit(solution)/shard_map/ppermute | solution.py:774
  288.5 3.6 %collective-permute-start.19 = (f32[1,1]{1,0:T(1,128)}, f32[1,1]{1,0:T(1,128)}, u32[]{:S(2)}, u32[]{:S(2)}) collective-permute-start(f32[1,1]{1,0:T(1,128)} %add.56), channel_id=1, source_target_pairs={{0,2},{1,3},{2,0},{3,1},{4,6},{5,7},{6,4},{7,5},{8,10},{9,11},{10,... | collective-permute-start | bytes 20 | tf_op jit(solution)/shard_map/ppermute | solution.py:774
  294.1 9.9 %collective-permute-start.23 = (f32[1,1]{1,0:T(1,128)}, f32[1,1]{1,0:T(1,128)}, u32[]{:S(2)}, u32[]{:S(2)}) collective-permute-start(f32[1,1]{1,0:T(1,128)} %add.59), channel_id=1, source_target_pairs={{0,16},{8,24},{16,0},{24,8},{1,17},{9,25},{17,1},{25,9},{2,18},{10... | collective-permute-start | bytes 20 | tf_op jit(solution)/shard_map/ppermute | solution.py:774
  296.9 7.0 %collective-permute-start.24 = (f32[1,1]{1,0:T(1,128)}, f32[1,1]{1,0:T(1,128)}, u32[]{:S(2)}, u32[]{:S(2)}) collective-permute-start(f32[1,1]{1,0:T(1,128)} %add.59), channel_id=1, source_target_pairs={{0,24},{8,16},{16,8},{24,0},{1,25},{9,17},{17,9},{25,1},{2,26},{10... | collective-permute-start | bytes 20 | tf_op jit(solution)/shard_map/ppermute | solution.py:774
  299.7 3.6 %collective-permute-start.22 = (f32[1,1]{1,0:T(1,128)}, f32[1,1]{1,0:T(1,128)}, u32[]{:S(2)}, u32[]{:S(2)}) collective-permute-start(f32[1,1]{1,0:T(1,128)} %add.59), channel_id=1, source_target_pairs={{0,8},{8,0},{16,24},{24,16},{1,9},{9,1},{17,25},{25,17},{2,10},{10... | collective-permute-start | bytes 20 | tf_op jit(solution)/shard_map/ppermute | solution.py:774
  (10 other events, 13.6 us)
Sparse Core Ops, SparseCore 0:
  59.2 99.8 all-gather.4
  172.9 45.9 all-gather.2
  221.2 57.9 reduce-scatter.3
